TPU v7x, 256 devices: a whole 4x4x8 slice. The times are simulated.
256 devices in a mesh: dp: 8 (over y, core), tensor: 32 (over x, z).
Axes of the slice: x: 4, y: 4, z: 8, core: 2. Of those that a mesh axis runs over, the one named last changes fastest.
Arguments:
- activations: bfloat16 [65536, 8192], P(('dp', 'tensor')), may hold values from -6 to 6
- cotangent: bfloat16 [65536, 1024], P(('dp', 'tensor')), may hold values from -6 to 6
- frozen_weight: bfloat16 [8192, 1024], P('tensor'), may hold values from -0.0625 to 0.0625
- adapter_down: bfloat16 [12, 8192, 64], P(None, 'tensor'), may hold values from -0.0625 to 0.0625
- adapter_up: bfloat16 [12, 64, 1024], replicated, may hold values from -0.75 to 0.75
- held_jobs: int32 [8, 3], P('dp'), may hold values from 0 to 11, as said below
- tile_slots: int32 [512], P(('dp', 'tensor')), may hold values from 0 to 2
- tile_lengths: int32 [512], P(('dp', 'tensor')), may hold values from 16 to 128
Outputs:
- grad_input: bfloat16 [65536, 8192], P(('dp', 'tensor'))
- grad_down: float32 [12, 8192, 64], P(None, 'tensor')
- grad_up: float32 [12, 64, 1024], replicated
Inputs may be any that keep to these rules, and one draw needn't show every extreme that they name: `held_jobs`: each row lists 3 different adapters, and every adapter appears in some row.
All inputs are finite; a program needn't handle non-finite values.
Results may differ from a plain program's by a relative error of at most 0.0046.
Values may be sent and summed in bfloat16 or wider, within the bound.
No kernel may reach another device: no remote copies, remote signals or barrier semaphores. Data moves between devices by JAX's collectives and lax.ppermute only.
A program may use at most 128 MiB of HBM per device.

v0:
```python
import functools
import jax
import jax.numpy as jnp
from jax import lax
from jax.experimental import pallas as pl
from jax.experimental.pallas import tpu as pltpu
from jax.sharding import Mesh, PartitionSpec as P

ADAPTER_SCALING = 2.0
NY, NCORE, NX, NZ = 4, 2, 4, 8
SWAP = [(0, 1), (1, 0)]
PAD = 128
F32, BF16 = jnp.float32, jnp.bfloat16
VMEM = pl.BlockSpec(memory_space=pltpu.VMEM)
SMEM = pl.BlockSpec(memory_space=pltpu.SMEM)
BIG = pltpu.CompilerParams(vmem_limit_bytes=56 * 1024 * 1024)


def shift(value, axis, size, by):
    return lax.ppermute(value, axis, [(i, (i + by) % size) for i in range(size)])


def ring_gather(block, axis, size, me):
    rows, columns = block.shape
    half = columns // 2
    whole = jnp.zeros((rows, size * columns), block.dtype)

    def put(whole, piece, owner, offset):
        return lax.dynamic_update_slice(whole, piece, (0, owner * columns + offset))

    whole = put(whole, block, me, 0)
    right = left = block
    for step in range(1, size // 2):
        right = shift(right, axis, size, 1)
        left = shift(left, axis, size, -1)
        whole = put(whole, right, (me - step) % size, 0)
        whole = put(whole, left, (me + step) % size, 0)
    far = (me + size // 2) % size
    whole = put(whole, shift(right[:, :half], axis, size, 1), far, 0)
    whole = put(whole, shift(left[:, half:], axis, size, -1), far, half)
    return whole


def tn(a, b):
    return lax.dot_general(a, b, (((0,), (0,)), ((), ())), preferred_element_type=F32)


def nt(a, b):
    return lax.dot_general(a, b, (((1,), (1,)), ((), ())), preferred_element_type=F32)


def nn(a, b):
    return lax.dot_general(a, b, (((1,), (0,)), ((), ())), preferred_element_type=F32)


def back_kernel(x, held, slots, lengths, act, cot, up, masked, back_slots, *terms):
    tiles = slots.shape[0]
    tile_rows = cot.shape[0] // tiles
    rank = up.shape[1]
    span = act.shape[1] // NX
    for tile in range(tiles):
        rows = pl.ds(tile * tile_rows, tile_rows)
        slot = slots[tile]
        row = lax.broadcasted_iota(jnp.int32, (tile_rows, 1), 0)
        live = jnp.where(row < lengths[tile], cot[rows, :], jnp.zeros((), BF16))
        masked[rows, :] = live
        back = nt(live, up[held[0, slot]]).astype(BF16)
        twice = back * jnp.asarray(ADAPTER_SCALING, BF16)
        for s in range(held.shape[1]):
            back_slots[rows, s * rank : (s + 1) * rank] = jnp.where(slot == s, twice, jnp.zeros((), BF16))
        ident = jnp.full((rank, PAD), slot.astype(F32), F32).astype(BF16)
        for by, out in enumerate(terms):
            columns = pl.ds(pl.multiple_of(lax.rem(x[0] + by, NX) * span, span), span)
            out[tile * rank : (tile + 1) * rank, :span] = tn(twice, act[rows, columns]).astype(BF16)
            out[tile * rank : (tile + 1) * rank, span:] = ident


def low_kernel(x, slots, act, masked, down, *terms):
    tiles = slots.shape[0]
    tile_rows = act.shape[0] // tiles
    rank = terms[0].shape[0] // tiles * NX
    deep = rank // NX
    for tile in range(tiles):
        rows = pl.ds(tile * tile_rows, tile_rows)
        mine = pl.ds(pl.multiple_of(slots[tile] * rank, rank), rank)
        low = nt(act[rows, :], down[mine, :]).astype(BF16)
        twice = low * jnp.asarray(ADAPTER_SCALING, BF16)
        term = tn(twice, masked[rows, :])
        for owner in range(NX):
            for by, out in enumerate(terms):
                @pl.when(lax.rem(x[0] + by, NX) == owner)
                def _():
                    out[tile * deep : (tile + 1) * deep, :] = term[owner * deep : (owner + 1) * deep, :]


def slot_kernel(slot_count, tiles, *refs):
    downs, ups, out = refs[:NX], refs[NX : 2 * NX], refs[2 * NX]
    rank = downs[0].shape[0] // tiles
    deep = ups[0].shape[0] // tiles
    share = out.shape[2]
    lanes = ups[0].shape[1] // NZ
    span = share * NZ
    idents = [
        [down[tile * rank : (tile + 1) * rank, span : span + PAD].astype(F32) for tile in range(tiles)]
        for down in downs
    ]
    top = slot_count * rank
    half = slot_count * deep // 2
    for z in range(NZ):
        ups_now = []
        for slot in range(slot_count):
            total = jnp.zeros((rank, share), F32)
            some = jnp.zeros((deep, lanes), F32)
            for down, up, ident in zip(downs, ups, idents):
                for tile in range(tiles):
                    part = down[tile * rank : (tile + 1) * rank, z * share : (z + 1) * share].astype(F32)
                    hit = ident[tile] == slot
                    wide = jnp.concatenate([hit] * (share // PAD), axis=1)
                    total = total + jnp.where(wide, part, 0.0)
                    part = up[tile * deep : (tile + 1) * deep, z * lanes : (z + 1) * lanes]
                    some = some + jnp.where(hit[:deep, :lanes], part, 0.0)
            out[z, slot * rank : (slot + 1) * rank, :] = total.astype(BF16)
            ups_now.append(some)
        ups_now = jnp.concatenate(ups_now, axis=0)
        rest = jnp.zeros((out.shape[1] - top - half, share), F32)
        packed = jnp.concatenate([ups_now[:half], ups_now[half:]], axis=1)
        out[z, top:, :] = jnp.concatenate([packed, rest], axis=0).astype(BF16)


def share_kernel(held, parts, out):
    total = parts[0].astype(F32)
    for z in range(1, NZ):
        total = total + parts[z].astype(F32)
    height = out.shape[0]
    row = lax.broadcasted_iota(jnp.int32, total.shape, 0)
    for s in range(held.shape[1]):
        total = jnp.where(row == height - held.shape[1] + s, held[0, s].astype(F32), total)
    out[...] = total.astype(BF16)


def job_kernel(slot_count, core, ids, parts, down, up, acc):
    jobs, rank, _ = down.shape
    deep = acc.shape[1]
    lanes = acc.shape[2]
    top = slot_count * rank
    half = slot_count * deep // 2
    down[...] = jnp.zeros_like(down)
    acc[...] = jnp.zeros_like(acc)
    for d in range(NY * NCORE):
        tail = parts[d, top:, :].astype(F32)
        ups = jnp.concatenate([tail[:half, :lanes], tail[:half, lanes:]], axis=0)
        for slot in range(slot_count):
            job = ids[d, slot]
            down[job] += parts[d, slot * rank : (slot + 1) * rank, :].astype(F32)
            acc[job] += ups[slot * deep : (slot + 1) * deep, :]
    some = jobs // NCORE
    for i in range(some):
        up[i * deep : (i + 1) * deep, :] = acc[core[0] * some + i].astype(BF16)


def spread_kernel(core, mine, other, out):
    some = out.shape[0] // NCORE
    deep = out.shape[1] // NX
    lanes = out.shape[2] // NZ
    for source, which in ((mine, core[0]), (other, 1 - core[0])):
        for i in range(some):
            for x in range(NX):
                row = [source[x, z, i * deep : (i + 1) * deep, :] for z in range(NZ)]
                out[which * some + i, x * deep : (x + 1) * deep, :] = jnp.concatenate(row, axis=1).astype(F32)


def input_kernel(core, masked, own, other, back_slots, down, out):
    half = own.shape[1]
    first = masked[:, :half]
    second = masked[:, half:]
    mine = jnp.where(core[0] == 0, first, second)
    theirs = jnp.where(core[0] == 0, second, first)
    total = nt(mine, own[...]) + nt(theirs, other[...]) + nn(back_slots[...], down[...])
    out[...] = total.astype(BF16)


def body(activations, cotangent, frozen_weight, adapter_down, adapter_up, held_jobs, tile_slots, tile_lengths):
    rows, width = activations.shape
    value_width = cotangent.shape[1]
    tiles = tile_slots.shape[0]
    jobs, rank = adapter_up.shape[0], adapter_up.shape[1]
    share = adapter_down.shape[1]
    held = held_jobs[0]
    slots = held.shape[0]
    span = width // NX
    deep = rank // NX
    lanes = value_width // NZ
    half = value_width // NCORE
    some = jobs // NCORE
    height = -(-(slots * rank + slots * deep // 2 + slots) // 32) * 32
    shape = jax.ShapeDtypeStruct
    core = lax.axis_index("core")
    x = lax.axis_index("x")
    z = lax.axis_index("z")
    core_at, x_at = core.reshape(1), x.reshape(1)

    with jax.named_scope("frozen_gather"):
        own_half = lax.dynamic_slice_in_dim(frozen_weight, core * half, half, 1)
        own_weight = lax.all_gather(own_half, ("x", "z"), axis=0, tiled=True)
        other_weight = lax.ppermute(own_weight, "core", SWAP)

    with jax.named_scope("down_gather"):
        down_mine = jnp.swapaxes(adapter_down, 1, 2)[held].reshape(slots * rank, share)
        down_z = ring_gather(down_mine, "z", NZ, z)
        down_all = ring_gather(down_z, "x", NX, x)

    with jax.named_scope("down_terms"):
        masked, back_slots, *down_terms = pl.pallas_call(
            back_kernel,
            out_shape=[shape((rows, value_width), BF16), shape((rows, slots * rank), BF16)]
            + [shape((tiles * rank, span + PAD), BF16)] * NX,
            in_specs=[SMEM] * 4 + [VMEM] * 3,
            out_specs=[VMEM] * (2 + NX),
            compiler_params=BIG,
        )(x_at, held_jobs, tile_slots, tile_lengths, activations, cotangent, adapter_up)
    with jax.named_scope("down_x"):
        down_got = [term if by == 0 else shift(term, "x", NX, by) for by, term in enumerate(down_terms)]

    with jax.named_scope("up_terms"):
        up_terms = pl.pallas_call(
            low_kernel,
            out_shape=[shape((tiles * deep, value_width), F32)] * NX,
            in_specs=[SMEM] * 2 + [VMEM] * 3,
            out_specs=[VMEM] * NX,
            compiler_params=BIG,
        )(x_at, tile_slots, activations, masked, down_all)
    with jax.named_scope("up_x"):
        up_got = [term if by == 0 else shift(term, "x", NX, by) for by, term in enumerate(up_terms)]

    with jax.named_scope("sum_x"):
        by_z = pl.pallas_call(
            functools.partial(slot_kernel, slots, tiles),
            out_shape=shape((NZ, height, share), BF16),
            in_specs=[VMEM] * (2 * NX),
            out_specs=VMEM,
            compiler_params=BIG,
        )(*down_got, *up_got)
    with jax.named_scope("exchange_z"):
        from_z = lax.all_to_all(by_z, "z", 0, 0, tiled=True)
    with jax.named_scope("sum_z"):
        mine = pl.pallas_call(
            share_kernel,
            out_shape=shape((height, share), BF16),
            in_specs=[SMEM, VMEM],
            out_specs=VMEM,
            compiler_params=BIG,
        )(held_jobs, from_z)
    with jax.named_scope("gather_dp"):
        groups = lax.all_gather(mine, ("y", "core"), axis=0, tiled=False)
        ids = groups[:, height - slots :, 0].astype(jnp.int32)
    with jax.named_scope("sum_dp"):
        grad_down, up_mine = pl.pallas_call(
            functools.partial(job_kernel, slots),
            out_shape=[shape((jobs, rank, share), F32), shape((some * deep, lanes), BF16)],
            in_specs=[SMEM, SMEM, VMEM],
            out_specs=[VMEM, VMEM],
            scratch_shapes=[pltpu.VMEM((jobs, deep, lanes), F32)],
            compiler_params=BIG,
        )(core_at, ids, groups)
        grad_down = jnp.swapaxes(grad_down, 1, 2)
    with jax.named_scope("up_spread"):
        line = lax.all_gather(up_mine, "z", axis=0, tiled=False)
        square = lax.all_gather(line, "x", axis=0, tiled=False)
        sibling = lax.ppermute(square, "core", SWAP)
        grad_up = pl.pallas_call(
            spread_kernel,
            out_shape=shape((jobs, rank, value_width), F32),
            in_specs=[SMEM, VMEM, VMEM],
            out_specs=VMEM,
            compiler_params=BIG,
        )(core_at, square, sibling)

    with jax.named_scope("grad_input"):
        block = 1024
        grad_input = pl.pallas_call(
            input_kernel,
            grid=(width // block,),
            out_shape=shape((rows, width), BF16),
            in_specs=[
                SMEM,
                pl.BlockSpec((rows, value_width), lambda i: (0, 0)),
                pl.BlockSpec((block, half), lambda i: (i, 0)),
                pl.BlockSpec((block, half), lambda i: (i, 0)),
                pl.BlockSpec((rows, slots * rank), lambda i: (0, 0)),
                pl.BlockSpec((slots * rank, block), lambda i: (0, i)),
            ],
            out_specs=pl.BlockSpec((rows, block), lambda i: (0, i)),
            compiler_params=BIG,
        )(core_at, masked, own_weight, other_weight, back_slots, down_all)
    return grad_input, grad_down, grad_up


def solution(mesh):
    fine = Mesh(mesh.devices.reshape(NY, NCORE, NX, NZ), ("y", "core", "x", "z"))
    dp, tensor, every = ("y", "core"), ("x", "z"), ("y", "core", "x", "z")
    return jax.shard_map(
        body,
        mesh=fine,
        in_specs=(
            P(every, None), P(every, None), P(tensor, None), P(None, tensor, None),
            P(), P(dp, None), P(every), P(every),
        ),
        out_specs=(P(every, None), P(None, tensor, None), P()),
        check_vma=False,
    )
```

profile of v0, /device:TPU:1, one launch (start us, length us, event | category | flops | bytes accessed | tf_op | source)
XLA Modules:
  0.0 320.9 jit_solution(6175517882040182199)
XLA Ops:
  7.2 0.0 copy-start
  7.2 0.0 all-gather.5.cloned.1.call-start
  7.2 1.0 copy-done
  8.2 0.7 constant_dynamic-slice_fusion
  8.9 0.0 all-gather.5.cloned.1.call-update
  9.0 103.9 %all-gather.5.cloned.1.call-done.own = bf16[8192,512]{1,0:T(8,128)(2,1)} async-done(((bf16[256,512]{1,0:T(8,128)(2,1)}), bf16[8192,512]{1,0:T(8,128)(2,1)}) %all-gather.5.cloned.1.call-update) | async-done | bytes 8388624 | tf_op jit(solution)/shard_map/frozen_gather/all_gather | solution.py:204
  112.9 1.1 collective-permute-start
  114.0 0.7 fusion
  114.6 1.5 gather_fusion
  116.2 0.1 collective-permute-start.1
  116.3 2.7 collective-permute-start.2
  118.9 0.1 broadcast_in_dim.8
  119.0 2.9 collective-permute-done.1
  121.9 0.0 collective-permute-start.3
  121.9 0.0 collective-permute-done.2
  121.9 2.7 collective-permute-start.4
  124.6 2.0 collective-permute-done.3
  126.6 0.0 collective-permute-start.5
  126.6 0.0 collective-permute-done.4
  126.6 2.7 collective-permute-start.6
  129.3 2.0 collective-permute-done.5
  131.3 0.0 collective-permute-start.7
  131.3 2.7 collective-permute-start.8
  134.1 1.4 collective-permute-done.7
  135.4 0.0 collective-permute-done.8
  135.5 0.1 collective-permute-start.9
  135.6 2.7 collective-permute-start.10
  138.2 5.5 %down_terms.1 = (bf16[256,1024]{1,0:T(8,128)(2,1)}, bf16[256,192]{1,0:T(8,128)(2,1)}, bf16[128,2176]{1,0:T(8,128)(2,1)}, bf16[128,2176]{1,0:T(8,128)(2,1)}, bf16...) custom-call(s32[1]{0:T(128)} %bitcast.1.x, s32[1,3]{1,0:T(1,128)} %held.3, s32[2]{0:T(128)} %slots.3, s32[2]{0:T(128)} %lengths.1, ...), custom_call_target="tpu_custom_call" | custom-call | tf_op jit(solution)/shard_map/down_terms/pallas_call | solution.py:213
  143.7 1.2 collective-permute-start.14
  144.9 6.6 %collective-permute-done.9 = bf16[192,2048]{1,0:T(8,128)(2,1)S(1)} collective-permute-done((bf16[192,2048]{1,0:T(8,128)(2,1)S(1)}, bf16[192,2048]{1,0:T(8,128)(2,1)S(1)}, u32[]{:S(2)}, u32[]{:S(2)}) %collective-permute-start.9) | collective-permute-done | bytes 786464 | tf_op jit(solution)/shard_map/down_gather/ppermute | solution.py:20
  151.6 0.3 collective-permute-start.11
  151.9 0.3 broadcast_in_dim.7
  152.2 0.1 constant_dynamic-update-slice_fusion.4
  152.3 3.0 collective-permute-start.12
  155.3 0.1 constant_dynamic-update-slice_fusion.3
  155.4 28.5 %collective-permute-done.11 = bf16[192,1024]{1,0:T(8,128)(2,1)S(1)} collective-permute-done((bf16[192,1024]{1,0:T(8,128)(2,1)S(1)}, bf16[192,1024]{1,0:T(8,128)(2,1)S(1)}, u32[]{:S(2)}, u32[]{:S(2)}) %collective-permute-start.11) | collective-permute-done | bytes 393248 | tf_op jit(solution)/shard_map/down_gather/ppermute | solution.py:20
  183.9 0.0 collective-permute-start.15
  183.9 0.1 constant_dynamic-update-slice_fusion.2
  184.0 1.6 copy-done.1
  185.7 7.3 %up_terms.1 = (f32[32,1024]{1,0:T(8,128)}, f32[32,1024]{1,0:T(8,128)}, f32[32,1024]{1,0:T(8,128)}, f32[32,1024]{1,0:T(8,128)}) custom-call(s32[1]{0:T(128)} %bitcast.1.x, s32[2]{0:T(128)} %slots.3, bf16[256,8192]{1,0:T(8,128)(2,1)} %act.3, bf16[256,1024]{1,0:T(8,128)(2,1)} %get-tuple-element.15.masked, bf16[192,8192]{1,0:T(8,128)(2,1)} %copy-done.1), custom_call_target="tpu_custom_call" | custom-call | tf_op jit(solution)/shard_map/up_terms/pallas_call | solution.py:225
  193.0 1.5 collective-permute-start.16
  194.5 0.0 collective-permute-done.14.refs_2_
  194.5 2.5 collective-permute-start.18
  197.0 0.0 collective-permute-done.15.refs_3_
  197.0 1.3 collective-permute-done.16.refs_5_
  198.3 1.8 collective-permute-done.17.refs_6_
  200.0 1.2 collective-permute-done.18.refs_7_
  201.3 0.6 copy-done.9
  201.9 4.2 %sum_x.1 = bf16[8,224,256]{2,1,0:T(8,128)(2,1)} custom-call(bf16[128,2176]{1,0:T(8,128)(2,1)} %get-tuple-element.17.refs_0_, bf16[128,2176]{1,0:T(8,128)(2,1)} %copy-done.5, bf16[128,2176]{1,0:T(8,128)(2,1)} %collective-permute-done.14.refs_2_, bf16[128,2176]{1,0:T(8,128)(2,1)} %copy-done.6, f32[32,1024]{1,0:T(8,128)} %get-tuple-element.21.refs_4_, ...), custom_call_target="tpu_custom_call" | custom-call | tf_op jit(solution)/shard_map/sum_x/pallas_call | solution.py:236
  206.0 23.7 %all_to_all.5.parts = bf16[8,224,256]{2,1,0:T(8,128)(2,1)} all-to-all(bf16[8,224,256]{2,1,0:T(8,128)(2,1)} %sum_x.1), channel_id=1, replica_groups=mesh['y'=4,'core'=2,'x'=4,'z'=8] {'z'}, dimensions={0} | all-to-all | bytes 1835008 | tf_op jit(solution)/shard_map/exchange_z/all_to_all | solution.py:244
  229.7 2.0 sum_z.1
  231.7 21.4 %all-gather = bf16[1792,256]{1,0:T(8,128)(2,1)S(1)} all-gather(bf16[224,256]{1,0:T(8,128)(2,1)} %sum_z.1), channel_id=2, replica_groups=mesh['y'=4,'core'=2,'x'=4,'z'=8] {'y','core'}, dimensions={0}, use_global_device_ids=true | all-gather | bytes 1032192 | tf_op jit(solution)/shard_map/gather_dp/all_gather | solution.py:254
  253.1 0.1 copy.15
  253.2 0.8 copy.16.ids
  253.9 0.0 copy-done.2
  254.0 2.3 sum_dp.1
  256.3 18.8 %all-gather.1 = bf16[768,128]{1,0:T(8,128)(2,1)S(1)} all-gather(bf16[96,128]{1,0:T(8,128)(2,1)} %get-tuple-element.26), channel_id=3, replica_groups=mesh['y'=4,'core'=2,'x'=4,'z'=8] {'z'}, dimensions={0}, use_global_device_ids=true | all-gather | bytes 221184 | tf_op jit(solution)/shard_map/up_spread/all_gather | solution.py:267
  275.0 10.4 %all-gather.2 = bf16[32,96,128]{2,1,0:T(8,128)(2,1)S(1)} all-gather(bf16[8,96,128]{2,1,0:T(8,128)(2,1)S(1)} %bitcast.17), channel_id=4, replica_groups=mesh['y'=4,'core'=2,'x'=4,'z'=8] {'x'}, dimensions={0}, use_global_device_ids=true | all-gather | bytes 983040 | tf_op jit(solution)/shard_map/up_spread/all_gather | solution.py:268
  285.5 9.2 %collective-permute-start.19 = (bf16[4,8,96,128]{3,2,1,0:T(8,128)(2,1)S(1)}, bf16[4,8,96,128]{3,2,1,0:T(8,128)(2,1)S(1)}, u32[]{:S(2)}, u32[]{:S(2)}) collective-permute-start(bf16[4,8,96,128]{3,2,1,0:T(8,128)(2,1)S(1)} %bitcast.15), channel_id=1, source_target_pairs={{0,32},{32,0},{1,33},{33,1},{2,34},{34,2},{3,35},{35,3},{4,36},{36... | collective-permute-start | bytes 2359304 | tf_op jit(solution)/shard_map/up_spread/ppermute | solution.py:269
  294.6 1.9 collective-permute-done.19.other
  296.5 0.9 copy-done.4
  297.4 3.2 %up_spread.1 = f32[12,64,1024]{2,1,0:T(8,128)} custom-call(s32[1]{0:T(128)} %bitcast.core, bf16[4,8,96,128]{3,2,1,0:T(8,128)(2,1)} %bitcast.16, bf16[4,8,96,128]{3,2,1,0:T(8,128)(2,1)} %copy-done.4), custom_call_target="tpu_custom_call" | custom-call | tf_op jit(solution)/shard_map/up_spread/pallas_call | solution.py:270
  300.7 0.0 collective-permute-done.other
  300.7 13.4 %grad_input.1 = bf16[256,8192]{1,0:T(8,128)(2,1)} custom-call(s32[1]{0:T(128)} %bitcast.core, bf16[256,1024]{1,0:T(8,128)(2,1)} %get-tuple-element.15.masked, bf16[8192,512]{1,0:T(8,128)(2,1)} %all-gather.5.cloned.1.call-done.own, bf16[8192,512]{1,0:T(8,128)(2,1)} %collective-permute-done.other, bf16[256,192]{1,0:T(8,128)(2,1)} %get-tuple-element.16.back_slots, ...), custom_call_target="tpu_custom_call" | custom-call | tf_op jit(solution)/shard_map/grad_input/pallas_call | solution.py:280
  (37 shorter events, 0.3 us)
Async XLA Ops:
  7.2 1.0 copy-start
  7.2 105.7 %all-gather.5.cloned.1.call-start = ((), (), s32[]{:S(2)}) async-start(), calls=%async_computation.1 | async-start | bytes 8650752 | tf_op jit(solution)/shard_map/frozen_gather/all_gather | solution.py:204
  112.9 187.8 %collective-permute-start = (bf16[8192,512]{1,0:T(8,128)(2,1)}, bf16[8192,512]{1,0:T(8,128)(2,1)}, u32[]{:S(2)}, u32[]{:S(2)}) collective-permute-start(bf16[8192,512]{1,0:T(8,128)(2,1)} %all-gather.5.cloned.1.call-done.own), channel_id=1, source_target_pairs={{0,32},{32,0},{1,33},{33,1},{2,34},{34,2},{3,35},{35,3},{4,36},{36... | collective-permute-start | bytes 25165832 | tf_op jit(solution)/shard_map/frozen_gather/ppermute | solution.py:205
  116.2 5.7 %collective-permute-start.1 = (bf16[192,256]{1,0:T(8,128)(2,1)S(1)}, bf16[192,256]{1,0:T(8,128)(2,1)S(1)}, u32[]{:S(2)}, u32[]{:S(2)}) collective-permute-start(bf16[192,256]{1,0:T(8,128)(2,1)S(1)} %bitcast.18), channel_id=1, source_target_pairs={{0,1},{1,2},{2,3},{3,4},{4,5},{5,6},{6,7},{7,0},{8,9},{9,10},{10,1... | collective-permute-start | bytes 294920 | tf_op jit(solution)/shard_map/down_gather/ppermute | solution.py:20
  116.3 5.6 %collective-permute-start.2 = (bf16[192,256]{1,0:T(8,128)(2,1)S(1)}, bf16[192,256]{1,0:T(8,128)(2,1)S(1)}, u32[]{:S(2)}, u32[]{:S(2)}) collective-permute-start(bf16[192,256]{1,0:T(8,128)(2,1)S(1)} %bitcast.19), channel_id=1, source_target_pairs={{0,7},{1,0},{2,1},{3,2},{4,3},{5,4},{6,5},{7,6},{8,15},{9,8},{10,9... | collective-permute-start | bytes 294920 | tf_op jit(solution)/shard_map/down_gather/ppermute | solution.py:20
  121.9 4.7 %collective-permute-start.3 = (bf16[192,256]{1,0:T(8,128)(2,1)S(1)}, bf16[192,256]{1,0:T(8,128)(2,1)S(1)}, u32[]{:S(2)}, u32[]{:S(2)}) collective-permute-start(bf16[192,256]{1,0:T(8,128)(2,1)S(1)} %collective-permute-done.1), channel_id=1, source_target_pairs={{0,1},{1,2},{2,3},{3,4},{4,5},{5,6},{6,7},{7,0},{8,9},{9,10},{10,1... | collective-permute-start | bytes 294920 | tf_op jit(solution)/shard_map/down_gather/ppermute | solution.py:20
  121.9 4.7 %collective-permute-start.4 = (bf16[192,256]{1,0:T(8,128)(2,1)S(1)}, bf16[192,256]{1,0:T(8,128)(2,1)S(1)}, u32[]{:S(2)}, u32[]{:S(2)}) collective-permute-start(bf16[192,256]{1,0:T(8,128)(2,1)S(1)} %collective-permute-done.2), channel_id=1, source_target_pairs={{0,7},{1,0},{2,1},{3,2},{4,3},{5,4},{6,5},{7,6},{8,15},{9,8},{10,9... | collective-permute-start | bytes 294920 | tf_op jit(solution)/shard_map/down_gather/ppermute | solution.py:20
  126.6 4.7 %collective-permute-start.5 = (bf16[192,256]{1,0:T(8,128)(2,1)S(1)}, bf16[192,256]{1,0:T(8,128)(2,1)S(1)}, u32[]{:S(2)}, u32[]{:S(2)}) collective-permute-start(bf16[192,256]{1,0:T(8,128)(2,1)S(1)} %collective-permute-done.3), channel_id=1, source_target_pairs={{0,1},{1,2},{2,3},{3,4},{4,5},{5,6},{6,7},{7,0},{8,9},{9,10},{10,1... | collective-permute-start | bytes 294920 | tf_op jit(solution)/shard_map/down_gather/ppermute | solution.py:20
  126.6 4.7 %collective-permute-start.6 = (bf16[192,256]{1,0:T(8,128)(2,1)S(1)}, bf16[192,256]{1,0:T(8,128)(2,1)S(1)}, u32[]{:S(2)}, u32[]{:S(2)}) collective-permute-start(bf16[192,256]{1,0:T(8,128)(2,1)S(1)} %collective-permute-done.4), channel_id=1, source_target_pairs={{0,7},{1,0},{2,1},{3,2},{4,3},{5,4},{6,5},{7,6},{8,15},{9,8},{10,9... | collective-permute-start | bytes 294920 | tf_op jit(solution)/shard_map/down_gather/ppermute | solution.py:20
  131.3 4.2 %collective-permute-start.7 = (bf16[192,128]{1,0:T(8,128)(2,1)S(1)}, bf16[192,128]{1,0:T(8,128)(2,1)S(1)}, u32[]{:S(2)}, u32[]{:S(2)}) collective-permute-start(bf16[192,128]{1,0:T(8,128)(2,1)S(1)} %slice.22), channel_id=1, source_target_pairs={{0,1},{1,2},{2,3},{3,4},{4,5},{5,6},{6,7},{7,0},{8,9},{9,10},{10,1... | collective-permute-start | bytes 147464 | tf_op jit(solution)/shard_map/down_gather/ppermute | solution.py:20
  131.3 4.1 %collective-permute-start.8 = (bf16[192,128]{1,0:T(8,128)(2,1)S(1)}, bf16[192,128]{1,0:T(8,128)(2,1)S(1)}, u32[]{:S(2)}, u32[]{:S(2)}) collective-permute-start(bf16[192,128]{1,0:T(8,128)(2,1)S(1)} %slice.23), channel_id=1, source_target_pairs={{0,7},{1,0},{2,1},{3,2},{4,3},{5,4},{6,5},{7,6},{8,15},{9,8},{10,9... | collective-permute-start | bytes 147464 | tf_op jit(solution)/shard_map/down_gather/ppermute | solution.py:20
  135.5 16.1 %collective-permute-start.9 = (bf16[192,2048]{1,0:T(8,128)(2,1)S(1)}, bf16[192,2048]{1,0:T(8,128)(2,1)S(1)}, u32[]{:S(2)}, u32[]{:S(2)}) collective-permute-start(bf16[192,2048]{1,0:T(8,128)(2,1)S(1)} %constant_dynamic-update-slice_fusion.5), channel_id=1, source_target_pairs={{0,8},{8,16},{16,24},{24,0},{1,9},{9,17},{17,25},{25,1},{2,10},{10... | collective-permute-start | bytes 2359304 | tf_op jit(solution)/shard_map/down_gather/ppermute | solution.py:20
  135.6 16.7 %collective-permute-start.10 = (bf16[192,2048]{1,0:T(8,128)(2,1)S(1)}, bf16[192,2048]{1,0:T(8,128)(2,1)S(1)}, u32[]{:S(2)}, u32[]{:S(2)}) collective-permute-start(bf16[192,2048]{1,0:T(8,128)(2,1)S(1)} %constant_dynamic-update-slice_fusion.5), channel_id=1, source_target_pairs={{0,24},{8,0},{16,8},{24,16},{1,25},{9,1},{17,9},{25,17},{2,26},{10... | collective-permute-start | bytes 2359304 | tf_op jit(solution)/shard_map/down_gather/ppermute | solution.py:20
  143.7 50.7 %collective-permute-start.13 = (bf16[128,2176]{1,0:T(8,128)(2,1)}, bf16[128,2176]{1,0:T(8,128)(2,1)S(1)}, u32[]{:S(2)}, u32[]{:S(2)}) collective-permute-start(bf16[128,2176]{1,0:T(8,128)(2,1)} %get-tuple-element.18), channel_id=1, source_target_pairs={{0,8},{8,16},{16,24},{24,0},{1,9},{9,17},{17,25},{25,1},{2,10},{10... | collective-permute-start | bytes 1671176 | tf_op jit(solution)/shard_map/down_x/ppermute | solution.py:20
  143.7 50.7 %collective-permute-start.14 = (bf16[128,2176]{1,0:T(8,128)(2,1)}, bf16[128,2176]{1,0:T(8,128)(2,1)}, u32[]{:S(2)}, u32[]{:S(2)}) collective-permute-start(bf16[128,2176]{1,0:T(8,128)(2,1)} %get-tuple-element.19), channel_id=1, source_target_pairs={{0,16},{8,24},{16,0},{24,8},{1,17},{9,25},{17,1},{25,9},{2,18},{10... | collective-permute-start | bytes 1671176 | tf_op jit(solution)/shard_map/down_x/ppermute | solution.py:20
  151.6 32.3 %collective-permute-start.11 = (bf16[192,1024]{1,0:T(8,128)(2,1)S(1)}, bf16[192,1024]{1,0:T(8,128)(2,1)S(1)}, u32[]{:S(2)}, u32[]{:S(2)}) collective-permute-start(bf16[192,1024]{1,0:T(8,128)(2,1)S(1)} %slice.24), channel_id=1, source_target_pairs={{0,8},{8,16},{16,24},{24,0},{1,9},{9,17},{17,25},{25,1},{2,10},{10... | collective-permute-start | bytes 1179656 | tf_op jit(solution)/shard_map/down_gather/ppermute | solution.py:20
  152.3 31.7 %collective-permute-start.12 = (bf16[192,1024]{1,0:T(8,128)(2,1)S(1)}, bf16[192,1024]{1,0:T(8,128)(2,1)S(1)}, u32[]{:S(2)}, u32[]{:S(2)}) collective-permute-start(bf16[192,1024]{1,0:T(8,128)(2,1)S(1)} %slice.25), channel_id=1, source_target_pairs={{0,24},{8,0},{16,8},{24,16},{1,25},{9,1},{17,9},{25,17},{2,26},{10... | collective-permute-start | bytes 1179656 | tf_op jit(solution)/shard_map/down_gather/ppermute | solution.py:20
  183.9 13.1 %collective-permute-start.15 = (bf16[128,2176]{1,0:T(8,128)(2,1)}, bf16[128,2176]{1,0:T(8,128)(2,1)S(1)}, u32[]{:S(2)}, u32[]{:S(2)}) collective-permute-start(bf16[128,2176]{1,0:T(8,128)(2,1)} %get-tuple-element.20), channel_id=1, source_target_pairs={{0,24},{8,0},{16,8},{24,16},{1,25},{9,1},{17,9},{25,17},{2,26},{10... | collective-permute-start | bytes 1671176 | tf_op jit(solution)/shard_map/down_x/ppermute | solution.py:20
  184.0 1.6 copy-start.1
  193.0 5.2 %collective-permute-start.16 = (f32[32,1024]{1,0:T(8,128)}, f32[32,1024]{1,0:T(8,128)S(1)}, u32[]{:S(2)}, u32[]{:S(2)}) collective-permute-start(f32[32,1024]{1,0:T(8,128)} %get-tuple-element.22), channel_id=1, source_target_pairs={{0,8},{8,16},{16,24},{24,0},{1,9},{9,17},{17,25},{25,1},{2,10},{10... | collective-permute-start | bytes 393224 | tf_op jit(solution)/shard_map/up_x/ppermute | solution.py:20
  194.5 6.8 %copy-start.5 = (bf16[128,2176]{1,0:T(8,128)(2,1)}, bf16[128,2176]{1,0:T(8,128)(2,1)S(1)}, u32[]{:S(2)}) copy-start(bf16[128,2176]{1,0:T(8,128)(2,1)S(1)} %collective-permute-done.13.refs_1_) | copy-start | bytes 1671172
  194.5 5.5 %collective-permute-start.17 = (f32[32,1024]{1,0:T(8,128)}, f32[32,1024]{1,0:T(8,128)S(1)}, u32[]{:S(2)}, u32[]{:S(2)}) collective-permute-start(f32[32,1024]{1,0:T(8,128)} %get-tuple-element.23), channel_id=1, source_target_pairs={{0,16},{8,24},{16,0},{24,8},{1,17},{9,25},{17,1},{25,9},{2,18},{10... | collective-permute-start | bytes 393224 | tf_op jit(solution)/shard_map/up_x/ppermute | solution.py:20
  194.5 6.7 %collective-permute-start.18 = (f32[32,1024]{1,0:T(8,128)}, f32[32,1024]{1,0:T(8,128)S(1)}, u32[]{:S(2)}, u32[]{:S(2)}) collective-permute-start(f32[32,1024]{1,0:T(8,128)} %get-tuple-element.24), channel_id=1, source_target_pairs={{0,24},{8,0},{16,8},{24,16},{1,25},{9,1},{17,9},{25,17},{2,26},{10... | collective-permute-start | bytes 393224 | tf_op jit(solution)/shard_map/up_x/ppermute | solution.py:20
  197.0 4.3 %copy-start.6 = (bf16[128,2176]{1,0:T(8,128)(2,1)}, bf16[128,2176]{1,0:T(8,128)(2,1)S(1)}, u32[]{:S(2)}) copy-start(bf16[128,2176]{1,0:T(8,128)(2,1)S(1)} %collective-permute-done.15.refs_3_) | copy-start | bytes 1671172
  198.3 3.0 copy-start.7
  200.0 1.2 copy-start.8
  201.2 0.6 copy-start.9
  253.1 0.9 copy-start.2
  285.5 11.1 %copy-start.3 = (bf16[32,96,128]{2,1,0:T(8,128)(2,1)}, bf16[32,96,128]{2,1,0:T(8,128)(2,1)S(1)}, u32[]{:S(2)}) copy-start(bf16[32,96,128]{2,1,0:T(8,128)(2,1)S(1)} %all-gather.2) | copy-start | bytes 2359300
  285.5 11.1 %collective-permute-start.19 = (bf16[4,8,96,128]{3,2,1,0:T(8,128)(2,1)S(1)}, bf16[4,8,96,128]{3,2,1,0:T(8,128)(2,1)S(1)}, u32[]{:S(2)}, u32[]{:S(2)}) collective-permute-start(bf16[4,8,96,128]{3,2,1,0:T(8,128)(2,1)S(1)} %bitcast.15), channel_id=1, source_target_pairs={{0,32},{32,0},{1,33},{33,1},{2,34},{34,2},{3,35},{35,3},{4,36},{36... | collective-permute-start | bytes 2359304 | tf_op jit(solution)/shard_map/up_spread/ppermute | solution.py:269
  296.5 0.9 copy-start.4
Sparse Core Ops, SparseCore 0:
  11.2 101.6 all-gather.4
where the time goes:
time: 321 us
  waiting for transfers between devices  153 us (48%)
  blocking collectives  74.3 us (23%)
  Pallas kernels  37.9 us (12%)
  starting transfers between devices  32.2 us (10%)
  between operations  14.3 us (4%)
  local copies, waits for them, and re-layouts  8.19 us (3%)
    all_gather x1, waiting for transfers between devices, body(): own_weight = lax.all_gather(own_half, ('x', 'z'), axis=0, tiled=True)  104 us
    ppermute x18, waiting for transfers between devices, shift(): lax.ppermute(value, axis, [(i, (i + by) % size) for i in range(size)])  47.5 us
    all_to_all x1, blocking collectives, body(): from_z = lax.all_to_all(by_z, 'z', 0, 0, tiled=True)  23.7 us
    ppermute x18, starting transfers between devices, shift(): lax.ppermute(value, axis, [(i, (i + by) % size) for i in range(size)])  22 us
    all_gather x1, blocking collectives, body(): groups = lax.all_gather(mine, ('y', 'core'), axis=0, tiled=False)  21.4 us
    all_gather x1, blocking collectives, body(): line = lax.all_gather(up_mine, 'z', axis=0, tiled=False)  18.8 us
    pallas_call x1, Pallas kernels, body(): pl.pallas_call(input_kernel, grid=(width // block,), out_shape=shape((row...  13.4 us
    all_gather x1, blocking collectives, body(): square = lax.all_gather(line, 'x', axis=0, tiled=False)  10.4 us
  transfers between devices with their start and end apart: 21, of which 11 were waited for; matrix products, arithmetic and copies ran while one was open for 1% of the time, Pallas kernels for 8%

commit v1 on v0

v1 whole, which is shorter than its diff:
```python
import functools
import jax
import jax.numpy as jnp
from jax import lax
from jax.experimental import pallas as pl
from jax.experimental.pallas import tpu as pltpu
from jax.sharding import Mesh, PartitionSpec as P

ADAPTER_SCALING = 2.0
NY, NCORE, NX, NZ = 4, 2, 4, 8
SWAP = [(0, 1), (1, 0)]
PAD = 128
F32, BF16 = jnp.float32, jnp.bfloat16
VMEM = pl.BlockSpec(memory_space=pltpu.VMEM)
SMEM = pl.BlockSpec(memory_space=pltpu.SMEM)
BIG = pltpu.CompilerParams(vmem_limit_bytes=56 * 1024 * 1024)


def cost(microseconds):
    return pl.CostEstimate(flops=0, transcendentals=0, bytes_accessed=int(microseconds * 3_000_000))


def shift(value, axis, size, by):
    return lax.ppermute(value, axis, [(i, (i + by) % size) for i in range(size)])


def after(value, event):
    return lax.optimization_barrier((value, event))[0]


def ring_gather(block, axis, size, me, second=None, last=None):
    rows, columns = block.shape
    half = columns // 2
    whole = jnp.zeros((rows, size * columns), block.dtype)

    def put(whole, piece, owner, offset):
        return lax.dynamic_update_slice(whole, piece, (0, owner * columns + offset))

    whole = put(whole, block, me, 0)
    right = left = block
    for step in range(1, size // 2):
        right = shift(right, axis, size, 1)
        left = shift(left, axis, size, -1)
        whole = put(whole, right, (me - step) % size, 0)
        whole = put(whole, left, (me + step) % size, 0)
        if step == 1 and second is not None:
            right, left = after((right, left), second)
    if last is not None:
        right, left = after((right, left), last)
    far = (me + size // 2) % size
    whole = put(whole, shift(right[:, :half], axis, size, 1), far, 0)
    whole = put(whole, shift(left[:, half:], axis, size, -1), far, half)
    return whole


def tn(a, b):
    return lax.dot_general(a, b, (((0,), (0,)), ((), ())), preferred_element_type=F32)


def nt(a, b):
    return lax.dot_general(a, b, (((1,), (1,)), ((), ())), preferred_element_type=F32)


def nn(a, b):
    return lax.dot_general(a, b, (((1,), (0,)), ((), ())), preferred_element_type=F32)


def back_kernel(x, held, slots, lengths, act, cot, up, masked, back_slots, *terms):
    tiles = slots.shape[0]
    tile_rows = cot.shape[0] // tiles
    rank = up.shape[1]
    span = act.shape[1] // NX
    for tile in range(tiles):
        rows = pl.ds(tile * tile_rows, tile_rows)
        slot = slots[tile]
        row = lax.broadcasted_iota(jnp.int32, (tile_rows, 1), 0)
        live = jnp.where(row < lengths[tile], cot[rows, :], jnp.zeros((), BF16))
        masked[rows, :] = live
        back = nt(live, up[held[0, slot]]).astype(BF16)
        twice = back * jnp.asarray(ADAPTER_SCALING, BF16)
        for s in range(held.shape[1]):
            back_slots[rows, s * rank : (s + 1) * rank] = jnp.where(slot == s, twice, jnp.zeros((), BF16))
        ident = jnp.full((rank, PAD), slot.astype(F32), F32).astype(BF16)
        for by, out in enumerate(terms):
            columns = pl.ds(pl.multiple_of(lax.rem(x[0] + by, NX) * span, span), span)
            out[tile * rank : (tile + 1) * rank, :span] = tn(twice, act[rows, columns]).astype(BF16)
            out[tile * rank : (tile + 1) * rank, span:] = ident


def low_kernel(held, slots, act, masked, down, out):
    tiles = slots.shape[0]
    tile_rows = act.shape[0] // tiles
    deep = 2 * NY * NCORE
    rank = NX * deep
    lanes = out.shape[2]
    terms, marks = [], []
    for tile in range(tiles):
        rows = pl.ds(tile * tile_rows, tile_rows)
        mine = pl.ds(pl.multiple_of(slots[tile] * rank, rank), rank)
        low = nt(act[rows, :], down[mine, :]).astype(BF16)
        twice = low * jnp.asarray(ADAPTER_SCALING, BF16)
        terms.append(tn(twice, masked[rows, :]))
        marks.append(jnp.full((2, lanes), held[0, slots[tile]].astype(F32), F32))
    for x in range(NX):
        for z in range(NZ):
            for d in range(NY * NCORE):
                first = x * deep + 2 * d
                cut = [term[first : first + 2, z * lanes : (z + 1) * lanes] for term in terms]
                out[(x * NZ + z) * NY * NCORE + d] = jnp.concatenate(cut + marks, axis=0).astype(BF16)


def up_job_kernel(jobs, downs, parts, out):
    value = parts[...].astype(F32)
    mark = pltpu.roll(value, 4, 1)
    sums = []
    for job in range(jobs):
        total = jnp.sum(jnp.where(mark == job, value, 0.0), axis=0)
        sums.append(total[0:2] + total[2:4])
    sums.append(jnp.zeros((32 - 2 * jobs, value.shape[2]), F32))
    sums = jnp.concatenate(sums, axis=0)
    top = downs.shape[0]
    out[:top, :] = downs[...]
    out[top:, :] = jnp.concatenate([sums[:16], sums[16:]], axis=1).astype(BF16)


def slot_kernel(slot_count, tiles, *refs):
    downs, out = refs[:NX], refs[NX]
    rank = downs[0].shape[0] // tiles
    share = out.shape[2]
    span = share * NZ
    idents = [
        [down[tile * rank : (tile + 1) * rank, span : span + PAD].astype(F32) for tile in range(tiles)]
        for down in downs
    ]
    for z in range(NZ):
        for slot in range(slot_count):
            total = jnp.zeros((rank, share), F32)
            for down, ident in zip(downs, idents):
                for tile in range(tiles):
                    part = down[tile * rank : (tile + 1) * rank, z * share : (z + 1) * share].astype(F32)
                    wide = jnp.concatenate([ident[tile] == slot] * (share // PAD), axis=1)
                    total = total + jnp.where(wide, part, 0.0)
            out[z, slot * rank : (slot + 1) * rank, :] = total.astype(BF16)


def share_kernel(held, parts, out):
    top = parts.shape[1]
    total = parts[0].astype(F32)
    for z in range(1, NZ):
        total = total + parts[z].astype(F32)
    out[:top, :] = total.astype(BF16)
    more = jnp.zeros((out.shape[0] - top, out.shape[1]), F32)
    row = lax.broadcasted_iota(jnp.int32, more.shape, 0)
    for s in range(held.shape[1]):
        more = jnp.where(row == s, held[0, s].astype(F32), more)
    out[top:, :] = more.astype(BF16)


def job_kernel(slot_count, ids, parts, down):
    rank = down.shape[1]
    down[...] = jnp.zeros_like(down)
    for d in range(NY * NCORE):
        for slot in range(slot_count):
            down[ids[d, slot]] += parts[d, slot * rank : (slot + 1) * rank, :].astype(F32)


def spread_kernel(core, mine, other, out):
    some = out.shape[0] // NCORE
    deep = out.shape[1] // NX
    for source, which in ((mine, core[0]), (other, 1 - core[0])):
        for x in range(NX):
            for i in range(some):
                line = [source[x * NZ + z, i * deep : (i + 1) * deep, :] for z in range(NZ)]
                out[which * some + i, x * deep : (x + 1) * deep, :] = jnp.concatenate(line, axis=1).astype(F32)


def input_kernel(masked, weight, back_slots, down, out):
    out[...] = (nt(masked[...], weight[...]) + nn(back_slots[...], down[...])).astype(BF16)


def body(activations, cotangent, frozen_weight, adapter_down, adapter_up, held_jobs, tile_slots, tile_lengths):
    rows, width = activations.shape
    value_width = cotangent.shape[1]
    tiles = tile_slots.shape[0]
    jobs, rank = adapter_up.shape[0], adapter_up.shape[1]
    share = adapter_down.shape[1]
    held = held_jobs[0]
    slots = held.shape[0]
    span = width // NX
    deep = rank // NX
    lanes = value_width // NZ
    some = jobs // NCORE
    shape = jax.ShapeDtypeStruct
    y = lax.axis_index("y")
    core = lax.axis_index("core")
    x = lax.axis_index("x")
    z = lax.axis_index("z")
    core_at, x_at = core.reshape(1), x.reshape(1)

    with jax.named_scope("frozen_gather"):
        part = frozen_weight.shape[0] // (NY * NCORE)
        own_part = lax.dynamic_slice_in_dim(frozen_weight, (y * NCORE + core) * part, part, 0)
        weight = lax.all_gather(own_part, ("x", "z", "y", "core"), axis=0, tiled=True)

    with jax.named_scope("down_terms"):
        masked, back_slots, *down_terms = pl.pallas_call(
            back_kernel,
            out_shape=[shape((rows, value_width), BF16), shape((rows, slots * rank), BF16)]
            + [shape((tiles * rank, span + PAD), BF16)] * NX,
            in_specs=[SMEM] * 4 + [VMEM] * 3,
            out_specs=[VMEM] * (2 + NX),
            compiler_params=BIG, cost_estimate=cost(5.5),
        )(x_at, held_jobs, tile_slots, tile_lengths, activations, cotangent, adapter_up)
    with jax.named_scope("down_x"):
        down_got = [term if by == 0 else shift(term, "x", NX, by) for by, term in enumerate(down_terms)]
    with jax.named_scope("down_sum_x"):
        down_by_z = pl.pallas_call(
            functools.partial(slot_kernel, slots, tiles),
            out_shape=shape((NZ, slots * rank, share), BF16),
            in_specs=[VMEM] * NX,
            out_specs=VMEM,
            compiler_params=BIG, cost_estimate=cost(4),
        )(*down_got)
    with jax.named_scope("down_z"):
        down_from_z = lax.all_to_all(down_by_z, "z", 0, 0, tiled=True)
    with jax.named_scope("down_sum_z"):
        mine = pl.pallas_call(
            share_kernel,
            out_shape=shape((slots * rank + 16, share), BF16),
            in_specs=[SMEM, VMEM],
            out_specs=VMEM,
            compiler_params=BIG, cost_estimate=cost(2),
        )(held_jobs, down_from_z)
    with jax.named_scope("down_gather"):
        down_mine = jnp.swapaxes(adapter_down, 1, 2)[held].reshape(slots * rank, share)
        down_z = ring_gather(down_mine, "z", NZ, z, second=down_terms)
        down_all = ring_gather(after(down_z, down_got), "x", NX, x)

    with jax.named_scope("up_terms"):
        receivers = NX * NZ * NY * NCORE
        up_terms = pl.pallas_call(
            low_kernel,
            out_shape=shape((receivers, 8, lanes), BF16),
            in_specs=[SMEM] * 2 + [VMEM] * 3,
            out_specs=VMEM,
            compiler_params=BIG, cost_estimate=cost(7),
        )(held_jobs, tile_slots, activations, masked, down_all)
    with jax.named_scope("up_all"):
        up_got = lax.all_to_all(up_terms, ("x", "z", "y", "core"), 0, 0, tiled=True)
    with jax.named_scope("up_sum"):
        packed = pl.pallas_call(
            functools.partial(up_job_kernel, jobs),
            out_shape=shape((slots * rank + 32, share), BF16),
            in_specs=[VMEM, VMEM],
            out_specs=VMEM,
            compiler_params=BIG, cost_estimate=cost(3),
        )(mine, up_got)
    with jax.named_scope("gather_dp"):
        groups = lax.all_gather(packed, ("y", "core"), axis=0, tiled=False)
        ids = groups[:, slots * rank : slots * rank + slots, 0].astype(jnp.int32)
    with jax.named_scope("down_dp"):
        grad_down = pl.pallas_call(
            functools.partial(job_kernel, slots),
            out_shape=shape((jobs, rank, share), F32),
            in_specs=[SMEM, VMEM],
            out_specs=VMEM,
            compiler_params=BIG, cost_estimate=cost(2.5),
        )(ids, groups)
    with jax.named_scope("up_spread"):
        ups = groups[:, slots * rank + 16 :]
        ups = jnp.concatenate([ups[:, :, :lanes], ups[:, :, lanes:]], axis=1)[:, : 2 * jobs]
        ups = ups.reshape(NY * NCORE, jobs, 2, lanes).transpose(1, 0, 2, 3)
        ups = lax.dynamic_slice_in_dim(ups, core * some, some, 0).reshape(some * deep, lanes)
        square = lax.all_to_all(jnp.broadcast_to(ups, (NX * NZ,) + ups.shape), ("x", "z"), 0, 0)
    with jax.named_scope("grad_input"):
        block = 1024
        grad_input = pl.pallas_call(
            input_kernel,
            grid=(width // block,),
            out_shape=shape((rows, width), BF16),
            in_specs=[
                pl.BlockSpec((rows, value_width), lambda i: (0, 0)),
                pl.BlockSpec((block, value_width), lambda i: (i, 0)),
                pl.BlockSpec((rows, slots * rank), lambda i: (0, 0)),
                pl.BlockSpec((slots * rank, block), lambda i: (0, i)),
            ],
            out_specs=pl.BlockSpec((rows, block), lambda i: (0, i)),
            compiler_params=BIG, cost_estimate=cost(13),
        )(masked, weight, back_slots, down_all)
    with jax.named_scope("up_swap"):
        sibling = lax.ppermute(after(square, grad_input), "core", SWAP)
        grad_up = pl.pallas_call(
            spread_kernel,
            out_shape=shape((jobs, rank, value_width), F32),
            in_specs=[SMEM, VMEM, VMEM],
            out_specs=VMEM,
            compiler_params=BIG, cost_estimate=cost(3),
        )(core_at, square, sibling)
    return grad_input, jnp.swapaxes(grad_down, 1, 2), grad_up


def solution(mesh):
    fine = Mesh(mesh.devices.reshape(NY, NCORE, NX, NZ), ("y", "core", "x", "z"))
    dp, tensor, every = ("y", "core"), ("x", "z"), ("y", "core", "x", "z")
    return jax.shard_map(
        body,
        mesh=fine,
        in_specs=(
            P(every, None), P(every, None), P(tensor, None), P(None, tensor, None),
            P(), P(dp, None), P(every), P(every),
        ),
        out_specs=(P(every, None), P(None, tensor, None), P()),
        check_vma=False,
    )
```

time: 321 us -> 193 us (0.60)
  waiting for transfers between devices: 153 us -> 57.6 us
  blocking collectives: 74.3 us -> 15.9 us
  starting transfers between devices: 32.2 us -> 51.8 us
  local copies, waits for them, and re-layouts: 8.19 us -> 11.6 us
    all_gather x1, waiting for transfers between devices: 104 us -> 0.02 us  [body(): lax.all_gather(own_part, ('x', 'z', 'y', 'core'), axis=0, tiled=True)]
    all_gather x3 -> x1, blocking collectives: 50.6 us -> 15.9 us  [body(): groups = lax.all_gather(packed, ('y', 'core'), axis=0, tiled=False)]
    all_to_all x0 -> x3, waiting for transfers between devices: none -> 28.3 us  [the longest x1 21.4 us: body(): up_got = lax.all_to_all(up_terms, ('x', 'z', 'y', 'core'), 0, 0, tiled=True)]
    all_to_all x0 -> x3, starting transfers between devices: none -> 23.9 us  [the longest x1 14.4 us: body(): up_got = lax.all_to_all(up_terms, ('x', 'z', 'y', 'core'), 0, 0, tiled=True)]
    all_to_all x1 -> x0, blocking collectives: 23.7 us -> none  [body(): from_z = lax.all_to_all(by_z, 'z', 0, 0, tiled=True)]
    ppermute x18 -> x15, waiting for transfers between devices: 47.5 us -> 29.3 us  [shift(): lax.ppermute(value, axis, [(i, (i + by) % size) for i in range(size)])]
    ppermute x2 -> x1, starting transfers between devices: 10.2 us -> 3.45 us  [body(): sibling = lax.ppermute(after(square, grad_input), 'core', SWAP)]
    pallas_call x3 -> x4, Pallas kernels: 11.6 us -> 14.4 us  [the longest x1 7.09 us: body(): pl.pallas_call(low_kernel, out_shape=shape((receivers, 8, lanes), BF16),...]
  transfers between devices with their start and end apart: 21 -> 20, of which waited for: 11 -> 8; matrix products, arithmetic and copies ran while one was open for 1% -> 4% of each run, Pallas kernels for 8% -> 19%
where the time goes in v1:
time: 193 us; the launch traced here: 192 us
  waiting for transfers between devices  57.6 us (30%)
  starting transfers between devices  51.8 us (27%)
  Pallas kernels  39.9 us (21%)
  blocking collectives  15.9 us (8%)
  between operations  14.4 us (7%)
  local copies, waits for them, and re-layouts  11.6 us (6%)
    ppermute x15, waiting for transfers between devices, shift(): lax.ppermute(value, axis, [(i, (i + by) % size) for i in range(size)])  29.3 us
    ppermute x15, starting transfers between devices, shift(): lax.ppermute(value, axis, [(i, (i + by) % size) for i in range(size)])  24.5 us
    all_to_all x1, waiting for transfers between devices, body(): up_got = lax.all_to_all(up_terms, ('x', 'z', 'y', 'core'), 0, 0, tiled=True)  21.4 us
    all_gather x1, blocking collectives, body(): groups = lax.all_gather(packed, ('y', 'core'), axis=0, tiled=False)  15.9 us
    all_to_all x1, starting transfers between devices, body(): up_got = lax.all_to_all(up_terms, ('x', 'z', 'y', 'core'), 0, 0, tiled=True)  14.4 us
    pallas_call x1, Pallas kernels, body(): pl.pallas_call(input_kernel, grid=(width // block,), out_shape=shape((row...  12.9 us
    pallas_call x1, Pallas kernels, body(): pl.pallas_call(low_kernel, out_shape=shape((receivers, 8, lanes), BF16),...  7.09 us
    all_to_all x1, waiting for transfers between devices, body(): lax.all_to_all(jnp.broadcast_to(ups, (NX * NZ,) + ups.shape), ('x', 'z'),...  6.88 us
  transfers between devices with their start and end apart: 20, of which 8 were waited for; matrix products, arithmetic and copies ran while one was open for 4% of the time, Pallas kernels for 19%

profile of v1, /device:TPU:1, one launch (start us, length us, event | category | flops | bytes accessed | tf_op | source)
XLA Modules:
  0.0 191.9 jit_solution(14150876618345303009)
XLA Ops:
  7.2 0.0 copy-start
  7.2 0.0 all-gather.3.cloned.1.call-start
  7.2 1.0 copy-done
  8.2 0.6 constant_dynamic-slice_fusion
  8.8 0.0 all-gather.3.cloned.1.call-update
  8.9 0.7 fusion
  9.5 1.5 gather_fusion
  11.1 2.5 %collective-permute-start = (bf16[192,256]{1,0:T(8,128)(2,1)S(1)}, bf16[192,256]{1,0:T(8,128)(2,1)S(1)}, u32[]{:S(2)}, u32[]{:S(2)}) collective-permute-start(bf16[192,256]{1,0:T(8,128)(2,1)S(1)} %bitcast.19), channel_id=1, source_target_pairs={{0,1},{1,2},{2,3},{3,4},{4,5},{5,6},{6,7},{7,0},{8,9},{9,10},{10,1... | collective-permute-start | bytes 294920 | tf_op jit(solution)/shard_map/down_gather/ppermute | solution.py:24
  13.6 4.0 %collective-permute-start.1 = (bf16[192,256]{1,0:T(8,128)(2,1)S(1)}, bf16[192,256]{1,0:T(8,128)(2,1)S(1)}, u32[]{:S(2)}, u32[]{:S(2)}) collective-permute-start(bf16[192,256]{1,0:T(8,128)(2,1)S(1)} %bitcast.20), channel_id=1, source_target_pairs={{0,7},{1,0},{2,1},{3,2},{4,3},{5,4},{6,5},{7,6},{8,15},{9,8},{10,9... | collective-permute-start | bytes 294920 | tf_op jit(solution)/shard_map/down_gather/ppermute | solution.py:24
  17.7 5.5 %down_terms.1 = (bf16[256,1024]{1,0:T(8,128)(2,1)}, bf16[256,192]{1,0:T(8,128)(2,1)}, bf16[128,2176]{1,0:T(8,128)(2,1)}, bf16[128,2176]{1,0:T(8,128)(2,1)}, bf16...) custom-call(s32[1]{0:T(128)} %bitcast.x, s32[1,3]{1,0:T(1,128)} %held.5, s32[2]{0:T(128)} %slots.3, s32[2]{0:T(128)} %lengths.1, ...), custom_call_target="tpu_custom_call" | custom-call | bytes 16500000 | tf_op jit(solution)/shard_map/down_terms/pallas_call | solution.py:206
  23.2 2.5 %collective-permute-start.10 = (bf16[128,2176]{1,0:T(8,128)(2,1)}, bf16[128,2176]{1,0:T(8,128)(2,1)S(1)}, u32[]{:S(2)}, u32[]{:S(2)}) collective-permute-start(bf16[128,2176]{1,0:T(8,128)(2,1)} %get-tuple-element.18), channel_id=1, source_target_pairs={{0,24},{8,0},{16,8},{24,16},{1,25},{9,1},{17,9},{25,17},{2,26},{10... | collective-permute-start | bytes 1671176 | tf_op jit(solution)/shard_map/down_x/ppermute | solution.py:24
  25.6 0.0 collective-permute-start.8
  25.7 1.7 collective-permute-start.9
  27.4 0.1 broadcast_in_dim.11
  27.5 0.0 collective-permute-done
  27.5 0.0 collective-permute-done.1
  27.5 0.1 collective-permute-start.2
  27.6 2.7 %collective-permute-start.3 = (bf16[192,256]{1,0:T(8,128)(2,1)S(1)}, bf16[192,256]{1,0:T(8,128)(2,1)S(1)}, u32[]{:S(2)}, u32[]{:S(2)}) collective-permute-start(bf16[192,256]{1,0:T(8,128)(2,1)S(1)} %collective-permute-done.1), channel_id=1, source_target_pairs={{0,7},{1,0},{2,1},{3,2},{4,3},{5,4},{6,5},{7,6},{8,15},{9,8},{10,9... | collective-permute-start | bytes 294920 | tf_op jit(solution)/shard_map/down_gather/ppermute | solution.py:24
  30.3 2.3 %collective-permute-done.2 = bf16[192,256]{1,0:T(8,128)(2,1)S(1)} collective-permute-done((bf16[192,256]{1,0:T(8,128)(2,1)S(1)}, bf16[192,256]{1,0:T(8,128)(2,1)S(1)}, u32[]{:S(2)}, u32[]{:S(2)}) %collective-permute-start.2) | collective-permute-done | bytes 98336 | tf_op jit(solution)/shard_map/down_gather/ppermute | solution.py:24
  32.6 0.0 collective-permute-start.4
  32.6 2.7 %collective-permute-start.5 = (bf16[192,256]{1,0:T(8,128)(2,1)S(1)}, bf16[192,256]{1,0:T(8,128)(2,1)S(1)}, u32[]{:S(2)}, u32[]{:S(2)}) collective-permute-start(bf16[192,256]{1,0:T(8,128)(2,1)S(1)} %collective-permute-done.3), channel_id=1, source_target_pairs={{0,7},{1,0},{2,1},{3,2},{4,3},{5,4},{6,5},{7,6},{8,15},{9,8},{10,9... | collective-permute-start | bytes 294920 | tf_op jit(solution)/shard_map/down_gather/ppermute | solution.py:24
  35.3 2.3 %collective-permute-done.4 = bf16[192,256]{1,0:T(8,128)(2,1)S(1)} collective-permute-done((bf16[192,256]{1,0:T(8,128)(2,1)S(1)}, bf16[192,256]{1,0:T(8,128)(2,1)S(1)}, u32[]{:S(2)}, u32[]{:S(2)}) %collective-permute-start.4) | collective-permute-done | bytes 98336 | tf_op jit(solution)/shard_map/down_gather/ppermute | solution.py:24
  37.6 0.0 collective-permute-start.6
  37.6 2.7 %collective-permute-start.7 = (bf16[192,128]{1,0:T(8,128)(2,1)S(1)}, bf16[192,128]{1,0:T(8,128)(2,1)S(1)}, u32[]{:S(2)}, u32[]{:S(2)}) collective-permute-start(bf16[192,128]{1,0:T(8,128)(2,1)S(1)} %slice.38), channel_id=1, source_target_pairs={{0,7},{1,0},{2,1},{3,2},{4,3},{5,4},{6,5},{7,6},{8,15},{9,8},{10,9... | collective-permute-start | bytes 147464 | tf_op jit(solution)/shard_map/down_gather/ppermute | solution.py:24
  40.4 1.7 collective-permute-done.6
  42.1 0.0 collective-permute-done.7
  42.2 0.0 collective-permute-done.8.refs_1_
  42.2 9.6 %collective-permute-done.9.refs_2_ = bf16[128,2176]{1,0:T(8,128)(2,1)} collective-permute-done((bf16[128,2176]{1,0:T(8,128)(2,1)}, bf16[128,2176]{1,0:T(8,128)(2,1)}, u32[]{:S(2)}, u32[]{:S(2)}) %collective-permute-start.9) | collective-permute-done | bytes 557088 | tf_op jit(solution)/shard_map/down_x/ppermute | solution.py:24
  51.8 0.0 collective-permute-start.11
  51.8 2.7 %collective-permute-start.12 = (bf16[192,2048]{1,0:T(8,128)(2,1)S(1)}, bf16[192,2048]{1,0:T(8,128)(2,1)}, u32[]{:S(2)}, u32[]{:S(2)}) collective-permute-start(bf16[192,2048]{1,0:T(8,128)(2,1)S(1)} %constant_dynamic-update-slice_fusion.5), channel_id=1, source_target_pairs={{0,24},{8,0},{16,8},{24,16},{1,25},{9,1},{17,9},{25,17},{2,26},{10... | collective-permute-start | bytes 2359304 | tf_op jit(solution)/shard_map/down_gather/ppermute | solution.py:24
  54.5 3.8 %down_sum_x.1 = bf16[8,192,256]{2,1,0:T(8,128)(2,1)} custom-call(bf16[128,2176]{1,0:T(8,128)(2,1)} %get-tuple-element.15.refs_0_, bf16[128,2176]{1,0:T(8,128)(2,1)} %copy-done.8, bf16[128,2176]{1,0:T(8,128)(2,1)} %collective-permute-done.9.refs_2_, bf16[128,2176]{1,0:T(8,128)(2,1)} %copy-done.7), custom_call_target="tpu_custom_call" | custom-call | bytes 12000000 | tf_op jit(solution)/shard_map/down_sum_x/pallas_call | solution.py:217
  58.3 4.9 %all-to-all-start = ((bf16[8,192,256]{2,1,0:T(8,128)(2,1)}), bf16[8,192,256]{2,1,0:T(8,128)(2,1)S(1)}, u32[]{:S(2)}, u32[]{:S(2)}) async-start(bf16[8,192,256]{2,1,0:T(8,128)(2,1)} %down_sum_x.1), calls=%async_computation | async-start | bytes 1572864 | tf_op jit(solution)/shard_map/down_z/all_to_all | solution.py:225
  63.2 0.3 broadcast_in_dim.10
  63.6 0.1 constant_dynamic-update-slice_fusion.4
  63.6 5.4 %collective-permute-done.11 = bf16[192,2048]{1,0:T(8,128)(2,1)S(1)} collective-permute-done((bf16[192,2048]{1,0:T(8,128)(2,1)S(1)}, bf16[192,2048]{1,0:T(8,128)(2,1)S(1)}, u32[]{:S(2)}, u32[]{:S(2)}) %collective-permute-start.11) | collective-permute-done | bytes 786464 | tf_op jit(solution)/shard_map/down_gather/ppermute | solution.py:24
  69.1 0.1 collective-permute-start.13
  69.2 0.0 collective-permute-done.12
  69.2 1.1 slice.40
  70.3 2.7 %collective-permute-start.14 = (bf16[192,1024]{1,0:T(8,128)(2,1)S(1)}, bf16[192,1024]{1,0:T(8,128)(2,1)S(1)}, u32[]{:S(2)}, u32[]{:S(2)}) collective-permute-start(bf16[192,1024]{1,0:T(8,128)(2,1)S(1)} %slice.40), channel_id=1, source_target_pairs={{0,24},{8,0},{16,8},{24,16},{1,25},{9,1},{17,9},{25,17},{2,26},{10... | collective-permute-start | bytes 1179656 | tf_op jit(solution)/shard_map/down_gather/ppermute | solution.py:24
  73.0 0.1 constant_dynamic-update-slice_fusion.3
  73.1 1.2 constant_dynamic-update-slice_fusion.2
  74.3 8.0 %collective-permute-done.13 = bf16[192,1024]{1,0:T(8,128)(2,1)S(1)} collective-permute-done((bf16[192,1024]{1,0:T(8,128)(2,1)S(1)}, bf16[192,1024]{1,0:T(8,128)(2,1)S(1)}, u32[]{:S(2)}, u32[]{:S(2)}) %collective-permute-start.13) | collective-permute-done | bytes 393248 | tf_op jit(solution)/shard_map/down_gather/ppermute | solution.py:24
  82.4 0.0 copy-start.1
  82.5 1.7 copy-done.1
  84.1 7.1 %up_terms.1 = bf16[256,8,128]{2,1,0:T(8,128)(2,1)} custom-call(s32[1,3]{1,0:T(1,128)} %held.5, s32[2]{0:T(128)} %slots.3, bf16[256,8192]{1,0:T(8,128)(2,1)} %act.3, bf16[256,1024]{1,0:T(8,128)(2,1)} %get-tuple-element.13.masked, bf16[192,8192]{1,0:T(8,128)(2,1)} %copy-done.1), custom_call_target="tpu_custom_call" | custom-call | bytes 21000000 | tf_op jit(solution)/shard_map/up_terms/pallas_call | solution.py:241
  91.2 0.0 all-to-all-done.parts
  91.2 14.4 %all-to-all-start.1 = ((bf16[256,8,128]{2,1,0:T(8,128)(2,1)}), bf16[256,8,128]{2,1,0:T(8,128)(2,1)S(1)}, u32[]{:S(2)}, u32[]{:S(2)}) async-start(bf16[256,8,128]{2,1,0:T(8,128)(2,1)} %up_terms.1), calls=%async_computation.1 | async-start | bytes 1048576 | tf_op jit(solution)/shard_map/up_all/all_to_all | solution.py:249
  105.6 1.9 down_sum_z.1.downs
  107.5 21.4 %all-to-all-done.1.parts = bf16[256,8,128]{2,1,0:T(8,128)(2,1)S(1)} async-done(((bf16[256,8,128]{2,1,0:T(8,128)(2,1)}), bf16[256,8,128]{2,1,0:T(8,128)(2,1)S(1)}, u32[]{:S(2)}, u32[]{:S(2)}) %all-to-all-start.1) | async-done | bytes 524320 | tf_op jit(solution)/shard_map/up_all/all_to_all | solution.py:249
  128.9 0.8 copy-done.5
  129.7 3.2 %up_sum.1 = bf16[224,256]{1,0:T(8,128)(2,1)} custom-call(bf16[208,256]{1,0:T(8,128)(2,1)} %down_sum_z.1.downs, bf16[256,8,128]{2,1,0:T(8,128)(2,1)} %copy-done.5), custom_call_target="tpu_custom_call" | custom-call | bytes 9000000 | tf_op jit(solution)/shard_map/up_sum/pallas_call | solution.py:251
  132.9 15.9 %all-gather = bf16[1792,256]{1,0:T(8,128)(2,1)S(1)} all-gather(bf16[224,256]{1,0:T(8,128)(2,1)} %up_sum.1), channel_id=2, replica_groups=mesh['y'=4,'core'=2,'x'=4,'z'=8] {'y','core'}, dimensions={0}, use_global_device_ids=true | all-gather | bytes 1032192 | tf_op jit(solution)/shard_map/gather_dp/all_gather | solution.py:259
  148.9 1.1 broadcast_in_dim.12
  150.0 4.6 %all-to-all-start.2 = ((bf16[32,96,128]{2,1,0:T(8,128)(2,1)}), bf16[32,96,128]{2,1,0:T(8,128)(2,1)S(1)}, u32[]{:S(2)}, u32[]{:S(2)}) async-start(bf16[32,96,128]{2,1,0:T(8,128)(2,1)} %broadcast_in_dim.12), calls=%async_computation.2 | async-start | bytes 1572864 | tf_op jit(solution)/shard_map/up_spread/all_to_all | solution.py:274
  154.6 0.0 all-gather.3.cloned.1.call-done.weight
  154.6 12.9 %grad_input.1 = bf16[256,8192]{1,0:T(8,128)(2,1)} custom-call(bf16[256,1024]{1,0:T(8,128)(2,1)} %get-tuple-element.13.masked, bf16[8192,1024]{1,0:T(8,128)(2,1)} %all-gather.3.cloned.1.call-done.weight, bf16[256,192]{1,0:T(8,128)(2,1)} %get-tuple-element.14.back_slots, bf16[192,8192]{1,0:T(8,128)(2,1)} %copy-done.1), custom_call_target="tpu_custom_call" | custom-call | bytes 39000000 | tf_op jit(solution)/shard_map/grad_input/pallas_call | solution.py:277
  167.5 6.9 %all-to-all-done.2.mine = bf16[32,96,128]{2,1,0:T(8,128)(2,1)S(1)} async-done(((bf16[32,96,128]{2,1,0:T(8,128)(2,1)}), bf16[32,96,128]{2,1,0:T(8,128)(2,1)S(1)}, u32[]{:S(2)}, u32[]{:S(2)}) %all-to-all-start.2) | async-done | bytes 786464 | tf_op jit(solution)/shard_map/up_spread/all_to_all | solution.py:274
  174.4 3.5 %collective-permute-start.15 = (bf16[32,96,128]{2,1,0:T(8,128)(2,1)S(1)}, bf16[32,96,128]{2,1,0:T(8,128)(2,1)S(1)}, u32[]{:S(2)}, u32[]{:S(2)}) collective-permute-start(bf16[32,96,128]{2,1,0:T(8,128)(2,1)S(1)} %all-to-all-done.2.mine), channel_id=1, source_target_pairs={{0,32},{32,0},{1,33},{33,1},{2,34},{34,2},{3,35},{35,3},{4,36},{36... | collective-permute-start | bytes 2359304 | tf_op jit(solution)/shard_map/up_swap/ppermute | solution.py:291
  177.9 0.1 copy.14
  178.0 0.7 copy.15.ids
  178.6 2.3 %down_dp.1 = f32[12,64,256]{2,1,0:T(8,128)} custom-call(s32[8,3]{1,0:T(8,128)} %copy.15.ids, bf16[8,224,256]{2,1,0:T(8,128)(2,1)} %bitcast.17), custom_call_target="tpu_custom_call" | custom-call | bytes 7500000 | tf_op jit(solution)/shard_map/down_dp/pallas_call | solution.py:262
  180.9 0.0 collective-permute-done.15.other
  180.9 0.9 copy-done.6
  181.8 3.2 %up_swap.1 = f32[12,64,1024]{2,1,0:T(8,128)} custom-call(s32[1]{0:T(128)} %bitcast.8.core, bf16[32,96,128]{2,1,0:T(8,128)(2,1)} %copy-done.3, bf16[32,96,128]{2,1,0:T(8,128)(2,1)} %copy-done.6), custom_call_target="tpu_custom_call" | custom-call | bytes 9000000 | tf_op jit(solution)/shard_map/up_swap/pallas_call | solution.py:292
  (36 shorter events, 0.4 us)
Async XLA Ops:
  7.2 1.0 copy-start
  7.2 147.4 %all-gather.3.cloned.1.call-start = ((), (), s32[]{:S(2)}) async-start(), calls=%async_computation.3 | async-start | bytes 16842752 | tf_op jit(solution)/shard_map/frozen_gather/all_gather | solution.py:203
  11.1 16.4 %collective-permute-start = (bf16[192,256]{1,0:T(8,128)(2,1)S(1)}, bf16[192,256]{1,0:T(8,128)(2,1)S(1)}, u32[]{:S(2)}, u32[]{:S(2)}) collective-permute-start(bf16[192,256]{1,0:T(8,128)(2,1)S(1)} %bitcast.19), channel_id=1, source_target_pairs={{0,1},{1,2},{2,3},{3,4},{4,5},{5,6},{6,7},{7,0},{8,9},{9,10},{10,1... | collective-permute-start | bytes 294920 | tf_op jit(solution)/shard_map/down_gather/ppermute | solution.py:24
  13.6 13.9 %collective-permute-start.1 = (bf16[192,256]{1,0:T(8,128)(2,1)S(1)}, bf16[192,256]{1,0:T(8,128)(2,1)S(1)}, u32[]{:S(2)}, u32[]{:S(2)}) collective-permute-start(bf16[192,256]{1,0:T(8,128)(2,1)S(1)} %bitcast.20), channel_id=1, source_target_pairs={{0,7},{1,0},{2,1},{3,2},{4,3},{5,4},{6,5},{7,6},{8,15},{9,8},{10,9... | collective-permute-start | bytes 294920 | tf_op jit(solution)/shard_map/down_gather/ppermute | solution.py:24
  23.2 19.0 %collective-permute-start.10 = (bf16[128,2176]{1,0:T(8,128)(2,1)}, bf16[128,2176]{1,0:T(8,128)(2,1)S(1)}, u32[]{:S(2)}, u32[]{:S(2)}) collective-permute-start(bf16[128,2176]{1,0:T(8,128)(2,1)} %get-tuple-element.18), channel_id=1, source_target_pairs={{0,24},{8,0},{16,8},{24,16},{1,25},{9,1},{17,9},{25,17},{2,26},{10... | collective-permute-start | bytes 1671176 | tf_op jit(solution)/shard_map/down_x/ppermute | solution.py:24
  25.6 16.5 %collective-permute-start.8 = (bf16[128,2176]{1,0:T(8,128)(2,1)}, bf16[128,2176]{1,0:T(8,128)(2,1)S(1)}, u32[]{:S(2)}, u32[]{:S(2)}) collective-permute-start(bf16[128,2176]{1,0:T(8,128)(2,1)} %get-tuple-element.16), channel_id=1, source_target_pairs={{0,8},{8,16},{16,24},{24,0},{1,9},{9,17},{17,25},{25,1},{2,10},{10... | collective-permute-start | bytes 1671176 | tf_op jit(solution)/shard_map/down_x/ppermute | solution.py:24
  25.7 26.1 %collective-permute-start.9 = (bf16[128,2176]{1,0:T(8,128)(2,1)}, bf16[128,2176]{1,0:T(8,128)(2,1)}, u32[]{:S(2)}, u32[]{:S(2)}) collective-permute-start(bf16[128,2176]{1,0:T(8,128)(2,1)} %get-tuple-element.17), channel_id=1, source_target_pairs={{0,16},{8,24},{16,0},{24,8},{1,17},{9,25},{17,1},{25,9},{2,18},{10... | collective-permute-start | bytes 1671176 | tf_op jit(solution)/shard_map/down_x/ppermute | solution.py:24
  27.5 5.1 %collective-permute-start.2 = (bf16[192,256]{1,0:T(8,128)(2,1)S(1)}, bf16[192,256]{1,0:T(8,128)(2,1)S(1)}, u32[]{:S(2)}, u32[]{:S(2)}) collective-permute-start(bf16[192,256]{1,0:T(8,128)(2,1)S(1)} %collective-permute-done), channel_id=1, source_target_pairs={{0,1},{1,2},{2,3},{3,4},{4,5},{5,6},{6,7},{7,0},{8,9},{9,10},{10,1... | collective-permute-start | bytes 294920 | tf_op jit(solution)/shard_map/down_gather/ppermute | solution.py:24
  27.6 5.0 %collective-permute-start.3 = (bf16[192,256]{1,0:T(8,128)(2,1)S(1)}, bf16[192,256]{1,0:T(8,128)(2,1)S(1)}, u32[]{:S(2)}, u32[]{:S(2)}) collective-permute-start(bf16[192,256]{1,0:T(8,128)(2,1)S(1)} %collective-permute-done.1), channel_id=1, source_target_pairs={{0,7},{1,0},{2,1},{3,2},{4,3},{5,4},{6,5},{7,6},{8,15},{9,8},{10,9... | collective-permute-start | bytes 294920 | tf_op jit(solution)/shard_map/down_gather/ppermute | solution.py:24
  32.6 5.0 %collective-permute-start.4 = (bf16[192,256]{1,0:T(8,128)(2,1)S(1)}, bf16[192,256]{1,0:T(8,128)(2,1)S(1)}, u32[]{:S(2)}, u32[]{:S(2)}) collective-permute-start(bf16[192,256]{1,0:T(8,128)(2,1)S(1)} %collective-permute-done.2), channel_id=1, source_target_pairs={{0,1},{1,2},{2,3},{3,4},{4,5},{5,6},{6,7},{7,0},{8,9},{9,10},{10,1... | collective-permute-start | bytes 294920 | tf_op jit(solution)/shard_map/down_gather/ppermute | solution.py:24
  32.6 5.0 %collective-permute-start.5 = (bf16[192,256]{1,0:T(8,128)(2,1)S(1)}, bf16[192,256]{1,0:T(8,128)(2,1)S(1)}, u32[]{:S(2)}, u32[]{:S(2)}) collective-permute-start(bf16[192,256]{1,0:T(8,128)(2,1)S(1)} %collective-permute-done.3), channel_id=1, source_target_pairs={{0,7},{1,0},{2,1},{3,2},{4,3},{5,4},{6,5},{7,6},{8,15},{9,8},{10,9... | collective-permute-start | bytes 294920 | tf_op jit(solution)/shard_map/down_gather/ppermute | solution.py:24
  37.6 4.5 %collective-permute-start.6 = (bf16[192,128]{1,0:T(8,128)(2,1)S(1)}, bf16[192,128]{1,0:T(8,128)(2,1)S(1)}, u32[]{:S(2)}, u32[]{:S(2)}) collective-permute-start(bf16[192,128]{1,0:T(8,128)(2,1)S(1)} %slice.37), channel_id=1, source_target_pairs={{0,1},{1,2},{2,3},{3,4},{4,5},{5,6},{6,7},{7,0},{8,9},{9,10},{10,1... | collective-permute-start | bytes 147464 | tf_op jit(solution)/shard_map/down_gather/ppermute | solution.py:24
  37.6 4.5 %collective-permute-start.7 = (bf16[192,128]{1,0:T(8,128)(2,1)S(1)}, bf16[192,128]{1,0:T(8,128)(2,1)S(1)}, u32[]{:S(2)}, u32[]{:S(2)}) collective-permute-start(bf16[192,128]{1,0:T(8,128)(2,1)S(1)} %slice.38), channel_id=1, source_target_pairs={{0,7},{1,0},{2,1},{3,2},{4,3},{5,4},{6,5},{7,6},{8,15},{9,8},{10,9... | collective-permute-start | bytes 147464 | tf_op jit(solution)/shard_map/down_gather/ppermute | solution.py:24
  42.1 12.3 %copy-start.7 = (bf16[128,2176]{1,0:T(8,128)(2,1)}, bf16[128,2176]{1,0:T(8,128)(2,1)S(1)}, u32[]{:S(2)}) copy-start(bf16[128,2176]{1,0:T(8,128)(2,1)S(1)} %collective-permute-done.10.refs_3_) | copy-start | bytes 1671172
  42.2 12.3 %copy-start.8 = (bf16[128,2176]{1,0:T(8,128)(2,1)}, bf16[128,2176]{1,0:T(8,128)(2,1)S(1)}, u32[]{:S(2)}) copy-start(bf16[128,2176]{1,0:T(8,128)(2,1)S(1)} %collective-permute-done.8.refs_1_) | copy-start | bytes 1671172
  51.8 17.3 %collective-permute-start.11 = (bf16[192,2048]{1,0:T(8,128)(2,1)S(1)}, bf16[192,2048]{1,0:T(8,128)(2,1)S(1)}, u32[]{:S(2)}, u32[]{:S(2)}) collective-permute-start(bf16[192,2048]{1,0:T(8,128)(2,1)S(1)} %constant_dynamic-update-slice_fusion.5), channel_id=1, source_target_pairs={{0,8},{8,16},{16,24},{24,0},{1,9},{9,17},{17,25},{25,1},{2,10},{10... | collective-permute-start | bytes 2359304 | tf_op jit(solution)/shard_map/down_gather/ppermute | solution.py:24
  51.8 17.4 %collective-permute-start.12 = (bf16[192,2048]{1,0:T(8,128)(2,1)S(1)}, bf16[192,2048]{1,0:T(8,128)(2,1)}, u32[]{:S(2)}, u32[]{:S(2)}) collective-permute-start(bf16[192,2048]{1,0:T(8,128)(2,1)S(1)} %constant_dynamic-update-slice_fusion.5), channel_id=1, source_target_pairs={{0,24},{8,0},{16,8},{24,16},{1,25},{9,1},{17,9},{25,17},{2,26},{10... | collective-permute-start | bytes 2359304 | tf_op jit(solution)/shard_map/down_gather/ppermute | solution.py:24
  58.3 32.9 %all-to-all-start = ((bf16[8,192,256]{2,1,0:T(8,128)(2,1)}), bf16[8,192,256]{2,1,0:T(8,128)(2,1)S(1)}, u32[]{:S(2)}, u32[]{:S(2)}) async-start(bf16[8,192,256]{2,1,0:T(8,128)(2,1)} %down_sum_x.1), calls=%async_computation | async-start | bytes 1572864 | tf_op jit(solution)/shard_map/down_z/all_to_all | solution.py:225
  69.1 13.2 %collective-permute-start.13 = (bf16[192,1024]{1,0:T(8,128)(2,1)S(1)}, bf16[192,1024]{1,0:T(8,128)(2,1)S(1)}, u32[]{:S(2)}, u32[]{:S(2)}) collective-permute-start(bf16[192,1024]{1,0:T(8,128)(2,1)S(1)} %slice.39), channel_id=1, source_target_pairs={{0,8},{8,16},{16,24},{24,0},{1,9},{9,17},{17,25},{25,1},{2,10},{10... | collective-permute-start | bytes 1179656 | tf_op jit(solution)/shard_map/down_gather/ppermute | solution.py:24
  70.3 12.1 %collective-permute-start.14 = (bf16[192,1024]{1,0:T(8,128)(2,1)S(1)}, bf16[192,1024]{1,0:T(8,128)(2,1)S(1)}, u32[]{:S(2)}, u32[]{:S(2)}) collective-permute-start(bf16[192,1024]{1,0:T(8,128)(2,1)S(1)} %slice.40), channel_id=1, source_target_pairs={{0,24},{8,0},{16,8},{24,16},{1,25},{9,1},{17,9},{25,17},{2,26},{10... | collective-permute-start | bytes 1179656 | tf_op jit(solution)/shard_map/down_gather/ppermute | solution.py:24
  82.4 1.7 copy-start.1
  91.2 14.4 %copy-start.4 = (bf16[8,192,256]{2,1,0:T(8,128)(2,1)}, bf16[8,192,256]{2,1,0:T(8,128)(2,1)S(1)}, u32[]{:S(2)}) copy-start(bf16[8,192,256]{2,1,0:T(8,128)(2,1)S(1)} %all-to-all-done.parts) | copy-start | bytes 2359300
  91.2 37.7 %all-to-all-start.1 = ((bf16[256,8,128]{2,1,0:T(8,128)(2,1)}), bf16[256,8,128]{2,1,0:T(8,128)(2,1)S(1)}, u32[]{:S(2)}, u32[]{:S(2)}) async-start(bf16[256,8,128]{2,1,0:T(8,128)(2,1)} %up_terms.1), calls=%async_computation.1 | async-start | bytes 1048576 | tf_op jit(solution)/shard_map/up_all/all_to_all | solution.py:249
  128.9 0.8 copy-start.5
  148.8 29.0 %copy-start.2 = (bf16[1792,256]{1,0:T(8,128)(2,1)}, bf16[1792,256]{1,0:T(8,128)(2,1)S(1)}, u32[]{:S(2)}) copy-start(bf16[1792,256]{1,0:T(8,128)(2,1)S(1)} %all-gather) | copy-start | bytes 2752516
  150.0 24.4 %all-to-all-start.2 = ((bf16[32,96,128]{2,1,0:T(8,128)(2,1)}), bf16[32,96,128]{2,1,0:T(8,128)(2,1)S(1)}, u32[]{:S(2)}, u32[]{:S(2)}) async-start(bf16[32,96,128]{2,1,0:T(8,128)(2,1)} %broadcast_in_dim.12), calls=%async_computation.2 | async-start | bytes 1572864 | tf_op jit(solution)/shard_map/up_spread/all_to_all | solution.py:274
  174.4 6.5 %copy-start.3 = (bf16[32,96,128]{2,1,0:T(8,128)(2,1)}, bf16[32,96,128]{2,1,0:T(8,128)(2,1)S(1)}, u32[]{:S(2)}) copy-start(bf16[32,96,128]{2,1,0:T(8,128)(2,1)S(1)} %all-to-all-done.2.mine) | copy-start | bytes 2359300
  174.4 6.5 %collective-permute-start.15 = (bf16[32,96,128]{2,1,0:T(8,128)(2,1)S(1)}, bf16[32,96,128]{2,1,0:T(8,128)(2,1)S(1)}, u32[]{:S(2)}, u32[]{:S(2)}) collective-permute-start(bf16[32,96,128]{2,1,0:T(8,128)(2,1)S(1)} %all-to-all-done.2.mine), channel_id=1, source_target_pairs={{0,32},{32,0},{1,33},{33,1},{2,34},{34,2},{3,35},{35,3},{4,36},{36... | collective-permute-start | bytes 2359304 | tf_op jit(solution)/shard_map/up_swap/ppermute | solution.py:291
  180.9 0.9 copy-start.6
Sparse Core Ops, SparseCore 0:
  11.7 140.4 all-gather.2

commit v2 on v1

--- a/solution.py
+++ b/solution.py
@@ -87,40 +87,51 @@
             out[tile * rank : (tile + 1) * rank, span:] = ident
 
 
-def low_kernel(held, slots, act, masked, down, out):
+def low_kernel(slots, act, masked, down, out):
     tiles = slots.shape[0]
     tile_rows = act.shape[0] // tiles
-    deep = 2 * NY * NCORE
+    lanes = out.shape[2]
+    deep = out.shape[1] // tiles - 16
     rank = NX * deep
-    lanes = out.shape[2]
     terms, marks = [], []
     for tile in range(tiles):
         rows = pl.ds(tile * tile_rows, tile_rows)
         mine = pl.ds(pl.multiple_of(slots[tile] * rank, rank), rank)
         low = nt(act[rows, :], down[mine, :]).astype(BF16)
         twice = low * jnp.asarray(ADAPTER_SCALING, BF16)
-        terms.append(tn(twice, masked[rows, :]))
-        marks.append(jnp.full((2, lanes), held[0, slots[tile]].astype(F32), F32))
-    for x in range(NX):
-        for z in range(NZ):
-            for d in range(NY * NCORE):
-                first = x * deep + 2 * d
-                cut = [term[first : first + 2, z * lanes : (z + 1) * lanes] for term in terms]
-                out[(x * NZ + z) * NY * NCORE + d] = jnp.concatenate(cut + marks, axis=0).astype(BF16)
-
-
-def up_job_kernel(jobs, downs, parts, out):
-    value = parts[...].astype(F32)
-    mark = pltpu.roll(value, 4, 1)
+        terms.append(tn(twice, masked[rows, :]).astype(BF16))
+        marks.append(jnp.full((16, lanes), slots[tile].astype(F32), F32).astype(BF16))
+    for to_x in range(NX):
+        for to_z in range(NZ):
+            for tile in range(tiles):
+                cut = terms[tile][to_x * deep : (to_x + 1) * deep, to_z * lanes : (to_z + 1) * lanes]
+                out[to_x * NZ + to_z, tile * deep : (tile + 1) * deep, :] = cut
+                first = tiles * deep + tile * 16
+                out[to_x * NZ + to_z, first : first + 16, :] = marks[tile]
+
+
+def up_sum_kernel(tiles, deep, held, downs, parts, out):
+    slot_count = held.shape[1]
+    lanes = parts.shape[2]
+    top = downs.shape[0]
     sums = []
-    for job in range(jobs):
-        total = jnp.sum(jnp.where(mark == job, value, 0.0), axis=0)
-        sums.append(total[0:2] + total[2:4])
-    sums.append(jnp.zeros((32 - 2 * jobs, value.shape[2]), F32))
+    for slot in range(slot_count):
+        total = jnp.zeros((deep, lanes), F32)
+        for source in range(parts.shape[0]):
+            for tile in range(tiles):
+                mark = parts[source, tiles * deep + tile * 16 : tiles * deep + (tile + 1) * 16, :].astype(F32)
+                part = parts[source, tile * deep : (tile + 1) * deep, :].astype(F32)
+                total = total + jnp.where(mark[:deep] == slot, part, 0.0)
+        sums.append(total)
     sums = jnp.concatenate(sums, axis=0)
-    top = downs.shape[0]
+    half = sums.shape[0] // 2
+    tail = jnp.concatenate([sums[:half], sums[half:]], axis=1)
+    tail = jnp.concatenate([tail, jnp.zeros((out.shape[0] - top - half, out.shape[1]), F32)], axis=0)
+    row = lax.broadcasted_iota(jnp.int32, tail.shape, 0)
+    for s in range(slot_count):
+        tail = jnp.where(row == tail.shape[0] - slot_count + s, held[0, s].astype(F32), tail)
     out[:top, :] = downs[...]
-    out[top:, :] = jnp.concatenate([sums[:16], sums[16:]], axis=1).astype(BF16)
+    out[top:, :] = tail.astype(BF16)
 
 
 def slot_kernel(slot_count, tiles, *refs):
@@ -143,25 +154,33 @@
             out[z, slot * rank : (slot + 1) * rank, :] = total.astype(BF16)
 
 
-def share_kernel(held, parts, out):
-    top = parts.shape[1]
+def share_kernel(parts, out):
     total = parts[0].astype(F32)
     for z in range(1, NZ):
         total = total + parts[z].astype(F32)
-    out[:top, :] = total.astype(BF16)
-    more = jnp.zeros((out.shape[0] - top, out.shape[1]), F32)
-    row = lax.broadcasted_iota(jnp.int32, more.shape, 0)
-    for s in range(held.shape[1]):
-        more = jnp.where(row == s, held[0, s].astype(F32), more)
-    out[top:, :] = more.astype(BF16)
-
-
-def job_kernel(slot_count, ids, parts, down):
-    rank = down.shape[1]
+    out[...] = total.astype(BF16)
+
+
+def job_kernel(slot_count, core, ids, parts, down, up, acc):
+    jobs, rank, _ = down.shape
+    deep = acc.shape[1]
+    lanes = acc.shape[2]
+    top = slot_count * rank
+    half = slot_count * deep // 2
     down[...] = jnp.zeros_like(down)
+    acc[...] = jnp.zeros_like(acc)
     for d in range(NY * NCORE):
+        tail = parts[d, top:, :].astype(F32)
+        ups = jnp.concatenate([tail[:half, :lanes], tail[:half, lanes:]], axis=0)
         for slot in range(slot_count):
-            down[ids[d, slot]] += parts[d, slot * rank : (slot + 1) * rank, :].astype(F32)
+            job = ids[d, slot]
+            down[job] += parts[d, slot * rank : (slot + 1) * rank, :].astype(F32)
+            acc[job] += ups[slot * deep : (slot + 1) * deep, :]
+    some = jobs // NCORE
+    for i in range(some):
+        mine = acc[core[0] * some + i].astype(BF16)
+        for copy in range(up.shape[0]):
+            up[copy, i * deep : (i + 1) * deep, :] = mine
 
 
 def spread_kernel(core, mine, other, out):
@@ -226,52 +245,48 @@
     with jax.named_scope("down_sum_z"):
         mine = pl.pallas_call(
             share_kernel,
-            out_shape=shape((slots * rank + 16, share), BF16),
-            in_specs=[SMEM, VMEM],
+            out_shape=shape((slots * rank, share), BF16),
+            in_specs=[VMEM],
             out_specs=VMEM,
             compiler_params=BIG, cost_estimate=cost(2),
-        )(held_jobs, down_from_z)
+        )(down_from_z)
     with jax.named_scope("down_gather"):
         down_mine = jnp.swapaxes(adapter_down, 1, 2)[held].reshape(slots * rank, share)
         down_z = ring_gather(down_mine, "z", NZ, z, second=down_terms)
         down_all = ring_gather(after(down_z, down_got), "x", NX, x)
 
     with jax.named_scope("up_terms"):
-        receivers = NX * NZ * NY * NCORE
         up_terms = pl.pallas_call(
             low_kernel,
-            out_shape=shape((receivers, 8, lanes), BF16),
-            in_specs=[SMEM] * 2 + [VMEM] * 3,
+            out_shape=shape((NX * NZ, tiles * (deep + 16), lanes), BF16),
+            in_specs=[SMEM] + [VMEM] * 3,
             out_specs=VMEM,
             compiler_params=BIG, cost_estimate=cost(7),
-        )(held_jobs, tile_slots, activations, masked, down_all)
-    with jax.named_scope("up_all"):
-        up_got = lax.all_to_all(up_terms, ("x", "z", "y", "core"), 0, 0, tiled=True)
+        )(tile_slots, activations, masked, down_all)
+    with jax.named_scope("up_tensor"):
+        up_got = lax.all_to_all(up_terms, ("x", "z"), 0, 0, tiled=True)
     with jax.named_scope("up_sum"):
         packed = pl.pallas_call(
-            functools.partial(up_job_kernel, jobs),
+            functools.partial(up_sum_kernel, tiles, deep),
             out_shape=shape((slots * rank + 32, share), BF16),
-            in_specs=[VMEM, VMEM],
-            out_specs=VMEM,
-            compiler_params=BIG, cost_estimate=cost(3),
-        )(mine, up_got)
+            in_specs=[SMEM, VMEM, VMEM],
+            out_specs=VMEM,
+            compiler_params=BIG, cost_estimate=cost(2),
+        )(held_jobs, mine, up_got)
     with jax.named_scope("gather_dp"):
         groups = lax.all_gather(packed, ("y", "core"), axis=0, tiled=False)
-        ids = groups[:, slots * rank : slots * rank + slots, 0].astype(jnp.int32)
-    with jax.named_scope("down_dp"):
-        grad_down = pl.pallas_call(
+        ids = groups[:, slots * rank + 32 - slots :, 0].astype(jnp.int32)
+    with jax.named_scope("sum_dp"):
+        grad_down, up_copies = pl.pallas_call(
             functools.partial(job_kernel, slots),
-            out_shape=shape((jobs, rank, share), F32),
-            in_specs=[SMEM, VMEM],
-            out_specs=VMEM,
+            out_shape=[shape((jobs, rank, share), F32), shape((NX * NZ, some * deep, lanes), BF16)],
+            in_specs=[SMEM, SMEM, VMEM],
+            out_specs=[VMEM, VMEM],
+            scratch_shapes=[pltpu.VMEM((jobs, deep, lanes), F32)],
             compiler_params=BIG, cost_estimate=cost(2.5),
-        )(ids, groups)
+        )(core_at, ids, groups)
     with jax.named_scope("up_spread"):
-        ups = groups[:, slots * rank + 16 :]
-        ups = jnp.concatenate([ups[:, :, :lanes], ups[:, :, lanes:]], axis=1)[:, : 2 * jobs]
-        ups = ups.reshape(NY * NCORE, jobs, 2, lanes).transpose(1, 0, 2, 3)
-        ups = lax.dynamic_slice_in_dim(ups, core * some, some, 0).reshape(some * deep, lanes)
-        square = lax.all_to_all(jnp.broadcast_to(ups, (NX * NZ,) + ups.shape), ("x", "z"), 0, 0)
+        square = lax.all_to_all(up_copies, ("x", "z"), 0, 0)
     with jax.named_scope("grad_input"):
         block = 1024
         grad_input = pl.pallas_call(

time: 193 us -> 182 us (0.943)
  waiting for transfers between devices: 57.6 us -> 47.7 us
  blocking collectives: 15.9 us -> 23.4 us
  starting transfers between devices: 51.8 us -> 46 us
    all_to_all x2, waiting for transfers between devices: 28.3 us -> 11.3 us  [the longest x1 9.5 us: body(): up_got = lax.all_to_all(up_terms, ('x', 'z'), 0, 0, tiled=True)]
    all_gather x1, blocking collectives: 15.9 us -> 23.4 us  [body(): groups = lax.all_gather(packed, ('y', 'core'), axis=0, tiled=False)]
    all_to_all x2, starting transfers between devices: 19 us -> 13.1 us  [the longest x1 6.97 us: body(): up_got = lax.all_to_all(up_terms, ('x', 'z'), 0, 0, tiled=True)]
    all_gather x1, waiting for transfers between devices: 0.02 us -> 5.15 us  [body(): lax.all_gather(own_part, ('x', 'z', 'y', 'core'), axis=0, tiled=True)]
  transfers between devices with their start and end apart: 20 -> 20, of which waited for: 8 -> 10; matrix products, arithmetic and copies ran while one was open for 4% -> 3% of each run, Pallas kernels for 19% -> 20%
where the time goes in v2:
time: 182 us; the launch traced here: 181 us
  waiting for transfers between devices  47.7 us (26%)
  starting transfers between devices  46 us (25%)
  Pallas kernels  38.9 us (21%)
  blocking collectives  23.4 us (13%)
  between operations  14.3 us (8%)
  local copies, waits for them, and re-layouts  10.5 us (6%)
    ppermute x15, waiting for transfers between devices, shift(): lax.ppermute(value, axis, [(i, (i + by) % size) for i in range(size)])  29.3 us
    ppermute x15, starting transfers between devices, shift(): lax.ppermute(value, axis, [(i, (i + by) % size) for i in range(size)])  24.5 us
    all_gather x1, blocking collectives, body(): groups = lax.all_gather(packed, ('y', 'core'), axis=0, tiled=False)  23.4 us
    pallas_call x1, Pallas kernels, body(): pl.pallas_call(input_kernel, grid=(width // block,), out_shape=shape((row...  12.9 us
    all_to_all x1, waiting for transfers between devices, body(): up_got = lax.all_to_all(up_terms, ('x', 'z'), 0, 0, tiled=True)  9.5 us
    all_to_all x1, starting transfers between devices, body(): up_got = lax.all_to_all(up_terms, ('x', 'z'), 0, 0, tiled=True)  6.97 us
    pallas_call x1, Pallas kernels, body(): pl.pallas_call(low_kernel, out_shape=shape((NX * NZ, tiles * (deep + 16),...  6.96 us
    all_to_all x1, starting transfers between devices, body(): square = lax.all_to_all(up_copies, ('x', 'z'), 0, 0)  6.14 us
  transfers between devices with their start and end apart: 20, of which 10 were waited for; matrix products, arithmetic and copies ran while one was open for 3% of the time, Pallas kernels for 20%

profile of v2, /device:TPU:1, one launch (start us, length us, event | category | flops | bytes accessed | tf_op | source)
XLA Modules:
  0.0 181.5 jit_solution(1185283695995007405)
XLA Ops:
  7.2 0.0 copy-start
  7.2 0.0 all-gather.3.cloned.1.call-start
  7.2 1.0 copy-done
  8.2 0.6 constant_dynamic-slice_fusion
  8.8 0.0 all-gather.3.cloned.1.call-update
  8.9 0.7 fusion
  9.5 1.5 gather_fusion
  11.1 2.5 %collective-permute-start = (bf16[192,256]{1,0:T(8,128)(2,1)S(1)}, bf16[192,256]{1,0:T(8,128)(2,1)S(1)}, u32[]{:S(2)}, u32[]{:S(2)}) collective-permute-start(bf16[192,256]{1,0:T(8,128)(2,1)S(1)} %bitcast.13), channel_id=1, source_target_pairs={{0,1},{1,2},{2,3},{3,4},{4,5},{5,6},{6,7},{7,0},{8,9},{9,10},{10,1... | collective-permute-start | bytes 294920 | tf_op jit(solution)/shard_map/down_gather/ppermute | solution.py:24
  13.6 4.0 %collective-permute-start.1 = (bf16[192,256]{1,0:T(8,128)(2,1)S(1)}, bf16[192,256]{1,0:T(8,128)(2,1)S(1)}, u32[]{:S(2)}, u32[]{:S(2)}) collective-permute-start(bf16[192,256]{1,0:T(8,128)(2,1)S(1)} %bitcast.14), channel_id=1, source_target_pairs={{0,7},{1,0},{2,1},{3,2},{4,3},{5,4},{6,5},{7,6},{8,15},{9,8},{10,9... | collective-permute-start | bytes 294920 | tf_op jit(solution)/shard_map/down_gather/ppermute | solution.py:24
  17.7 5.5 %down_terms.1 = (bf16[256,1024]{1,0:T(8,128)(2,1)}, bf16[256,192]{1,0:T(8,128)(2,1)}, bf16[128,2176]{1,0:T(8,128)(2,1)}, bf16[128,2176]{1,0:T(8,128)(2,1)}, bf16...) custom-call(s32[1]{0:T(128)} %bitcast.x, s32[1,3]{1,0:T(1,128)} %held.3, s32[2]{0:T(128)} %slots.3, s32[2]{0:T(128)} %lengths.1, ...), custom_call_target="tpu_custom_call" | custom-call | bytes 16500000 | tf_op jit(solution)/shard_map/down_terms/pallas_call | solution.py:225
  23.2 2.5 %collective-permute-start.10 = (bf16[128,2176]{1,0:T(8,128)(2,1)}, bf16[128,2176]{1,0:T(8,128)(2,1)S(1)}, u32[]{:S(2)}, u32[]{:S(2)}) collective-permute-start(bf16[128,2176]{1,0:T(8,128)(2,1)} %get-tuple-element.20), channel_id=1, source_target_pairs={{0,24},{8,0},{16,8},{24,16},{1,25},{9,1},{17,9},{25,17},{2,26},{10... | collective-permute-start | bytes 1671176 | tf_op jit(solution)/shard_map/down_x/ppermute | solution.py:24
  25.6 0.0 collective-permute-start.8
  25.7 1.7 collective-permute-start.9
  27.4 0.1 broadcast_in_dim.8
  27.5 0.0 collective-permute-done.1
  27.5 0.1 collective-permute-start.2
  27.6 2.7 %collective-permute-start.3 = (bf16[192,256]{1,0:T(8,128)(2,1)S(1)}, bf16[192,256]{1,0:T(8,128)(2,1)S(1)}, u32[]{:S(2)}, u32[]{:S(2)}) collective-permute-start(bf16[192,256]{1,0:T(8,128)(2,1)S(1)} %collective-permute-done.1), channel_id=1, source_target_pairs={{0,7},{1,0},{2,1},{3,2},{4,3},{5,4},{6,5},{7,6},{8,15},{9,8},{10,9... | collective-permute-start | bytes 294920 | tf_op jit(solution)/shard_map/down_gather/ppermute | solution.py:24
  30.3 2.3 %collective-permute-done.2 = bf16[192,256]{1,0:T(8,128)(2,1)S(1)} collective-permute-done((bf16[192,256]{1,0:T(8,128)(2,1)S(1)}, bf16[192,256]{1,0:T(8,128)(2,1)S(1)}, u32[]{:S(2)}, u32[]{:S(2)}) %collective-permute-start.2) | collective-permute-done | bytes 98336 | tf_op jit(solution)/shard_map/down_gather/ppermute | solution.py:24
  32.6 0.0 collective-permute-start.4
  32.6 0.0 collective-permute-done.3
  32.6 2.7 %collective-permute-start.5 = (bf16[192,256]{1,0:T(8,128)(2,1)S(1)}, bf16[192,256]{1,0:T(8,128)(2,1)S(1)}, u32[]{:S(2)}, u32[]{:S(2)}) collective-permute-start(bf16[192,256]{1,0:T(8,128)(2,1)S(1)} %collective-permute-done.3), channel_id=1, source_target_pairs={{0,7},{1,0},{2,1},{3,2},{4,3},{5,4},{6,5},{7,6},{8,15},{9,8},{10,9... | collective-permute-start | bytes 294920 | tf_op jit(solution)/shard_map/down_gather/ppermute | solution.py:24
  35.3 2.3 %collective-permute-done.4 = bf16[192,256]{1,0:T(8,128)(2,1)S(1)} collective-permute-done((bf16[192,256]{1,0:T(8,128)(2,1)S(1)}, bf16[192,256]{1,0:T(8,128)(2,1)S(1)}, u32[]{:S(2)}, u32[]{:S(2)}) %collective-permute-start.4) | collective-permute-done | bytes 98336 | tf_op jit(solution)/shard_map/down_gather/ppermute | solution.py:24
  37.6 0.0 collective-permute-done.5
  37.6 2.7 %collective-permute-start.7 = (bf16[192,128]{1,0:T(8,128)(2,1)S(1)}, bf16[192,128]{1,0:T(8,128)(2,1)S(1)}, u32[]{:S(2)}, u32[]{:S(2)}) collective-permute-start(bf16[192,128]{1,0:T(8,128)(2,1)S(1)} %slice.23), channel_id=1, source_target_pairs={{0,7},{1,0},{2,1},{3,2},{4,3},{5,4},{6,5},{7,6},{8,15},{9,8},{10,9... | collective-permute-start | bytes 147464 | tf_op jit(solution)/shard_map/down_gather/ppermute | solution.py:24
  40.4 1.7 collective-permute-done.6
  42.1 0.0 collective-permute-done.7
  42.1 0.0 collective-permute-done.10.refs_3_
  42.2 9.6 %collective-permute-done.9.refs_2_ = bf16[128,2176]{1,0:T(8,128)(2,1)} collective-permute-done((bf16[128,2176]{1,0:T(8,128)(2,1)}, bf16[128,2176]{1,0:T(8,128)(2,1)}, u32[]{:S(2)}, u32[]{:S(2)}) %collective-permute-start.9) | collective-permute-done | bytes 557088 | tf_op jit(solution)/shard_map/down_x/ppermute | solution.py:24
  51.8 0.0 collective-permute-start.11
  51.8 2.7 %collective-permute-start.12 = (bf16[192,2048]{1,0:T(8,128)(2,1)S(1)}, bf16[192,2048]{1,0:T(8,128)(2,1)}, u32[]{:S(2)}, u32[]{:S(2)}) collective-permute-start(bf16[192,2048]{1,0:T(8,128)(2,1)S(1)} %constant_dynamic-update-slice_fusion.5), channel_id=1, source_target_pairs={{0,24},{8,0},{16,8},{24,16},{1,25},{9,1},{17,9},{25,17},{2,26},{10... | collective-permute-start | bytes 2359304 | tf_op jit(solution)/shard_map/down_gather/ppermute | solution.py:24
  54.5 3.8 %down_sum_x.1 = bf16[8,192,256]{2,1,0:T(8,128)(2,1)} custom-call(bf16[128,2176]{1,0:T(8,128)(2,1)} %get-tuple-element.17.refs_0_, bf16[128,2176]{1,0:T(8,128)(2,1)} %copy-done.8, bf16[128,2176]{1,0:T(8,128)(2,1)} %collective-permute-done.9.refs_2_, bf16[128,2176]{1,0:T(8,128)(2,1)} %copy-done.7), custom_call_target="tpu_custom_call" | custom-call | bytes 12000000 | tf_op jit(solution)/shard_map/down_sum_x/pallas_call | solution.py:236
  58.3 4.9 %all-to-all-start = ((bf16[8,192,256]{2,1,0:T(8,128)(2,1)}), bf16[8,192,256]{2,1,0:T(8,128)(2,1)S(1)}, u32[]{:S(2)}, u32[]{:S(2)}) async-start(bf16[8,192,256]{2,1,0:T(8,128)(2,1)} %down_sum_x.1), calls=%async_computation | async-start | bytes 1572864 | tf_op jit(solution)/shard_map/down_z/all_to_all | solution.py:244
  63.2 0.3 broadcast_in_dim.7
  63.6 0.1 constant_dynamic-update-slice_fusion.4
  63.6 5.4 %collective-permute-done.11 = bf16[192,2048]{1,0:T(8,128)(2,1)S(1)} collective-permute-done((bf16[192,2048]{1,0:T(8,128)(2,1)S(1)}, bf16[192,2048]{1,0:T(8,128)(2,1)S(1)}, u32[]{:S(2)}, u32[]{:S(2)}) %collective-permute-start.11) | collective-permute-done | bytes 786464 | tf_op jit(solution)/shard_map/down_gather/ppermute | solution.py:24
  69.1 0.1 collective-permute-start.13
  69.2 1.1 slice.25
  70.3 2.7 %collective-permute-start.14 = (bf16[192,1024]{1,0:T(8,128)(2,1)S(1)}, bf16[192,1024]{1,0:T(8,128)(2,1)S(1)}, u32[]{:S(2)}, u32[]{:S(2)}) collective-permute-start(bf16[192,1024]{1,0:T(8,128)(2,1)S(1)} %slice.25), channel_id=1, source_target_pairs={{0,24},{8,0},{16,8},{24,16},{1,25},{9,1},{17,9},{25,17},{2,26},{10... | collective-permute-start | bytes 1179656 | tf_op jit(solution)/shard_map/down_gather/ppermute | solution.py:24
  73.0 0.1 constant_dynamic-update-slice_fusion.3
  73.1 1.2 constant_dynamic-update-slice_fusion.2
  74.3 8.0 %collective-permute-done.13 = bf16[192,1024]{1,0:T(8,128)(2,1)S(1)} collective-permute-done((bf16[192,1024]{1,0:T(8,128)(2,1)S(1)}, bf16[192,1024]{1,0:T(8,128)(2,1)S(1)}, u32[]{:S(2)}, u32[]{:S(2)}) %collective-permute-start.13) | collective-permute-done | bytes 393248 | tf_op jit(solution)/shard_map/down_gather/ppermute | solution.py:24
  82.4 0.0 collective-permute-done.14
  82.4 0.0 copy-start.1
  82.5 1.7 copy-done.1
  84.1 7.0 %up_terms.1 = bf16[32,64,128]{2,1,0:T(8,128)(2,1)} custom-call(s32[2]{0:T(128)} %slots.3, bf16[256,8192]{1,0:T(8,128)(2,1)} %act.3, bf16[256,1024]{1,0:T(8,128)(2,1)} %get-tuple-element.15.masked, bf16[192,8192]{1,0:T(8,128)(2,1)} %copy-done.1), custom_call_target="tpu_custom_call" | custom-call | bytes 21000000 | tf_op jit(solution)/shard_map/up_terms/pallas_call | solution.py:259
  91.1 0.0 all-to-all-done.parts
  91.1 7.0 %all-to-all-start.1 = ((bf16[32,64,128]{2,1,0:T(8,128)(2,1)}), bf16[32,64,128]{2,1,0:T(8,128)(2,1)S(1)}, u32[]{:S(2)}, u32[]{:S(2)}) async-start(bf16[32,64,128]{2,1,0:T(8,128)(2,1)} %up_terms.1), calls=%async_computation.1 | async-start | bytes 1048576 | tf_op jit(solution)/shard_map/up_tensor/all_to_all | solution.py:267
  98.1 1.9 %down_sum_z.1.downs = bf16[192,256]{1,0:T(8,128)(2,1)} custom-call(bf16[8,192,256]{2,1,0:T(8,128)(2,1)} %copy-done.4), custom_call_target="tpu_custom_call" | custom-call | bytes 6000000 | tf_op jit(solution)/shard_map/down_sum_z/pallas_call | solution.py:246
  99.9 9.5 %all-to-all-done.1.parts = bf16[32,64,128]{2,1,0:T(8,128)(2,1)S(1)} async-done(((bf16[32,64,128]{2,1,0:T(8,128)(2,1)}), bf16[32,64,128]{2,1,0:T(8,128)(2,1)S(1)}, u32[]{:S(2)}, u32[]{:S(2)}) %all-to-all-start.1) | async-done | bytes 524320 | tf_op jit(solution)/shard_map/up_tensor/all_to_all | solution.py:267
  109.5 0.8 copy-done.5
  110.2 2.0 %up_sum.1 = bf16[224,256]{1,0:T(8,128)(2,1)} custom-call(s32[1,3]{1,0:T(1,128)} %held.3, bf16[192,256]{1,0:T(8,128)(2,1)} %down_sum_z.1.downs, bf16[32,64,128]{2,1,0:T(8,128)(2,1)} %copy-done.5), custom_call_target="tpu_custom_call" | custom-call | bytes 6000000 | tf_op jit(solution)/shard_map/up_sum/pallas_call | solution.py:269
  112.2 23.4 %all-gather = bf16[1792,256]{1,0:T(8,128)(2,1)S(1)} all-gather(bf16[224,256]{1,0:T(8,128)(2,1)} %up_sum.1), channel_id=2, replica_groups=mesh['y'=4,'core'=2,'x'=4,'z'=8] {'y','core'}, dimensions={0}, use_global_device_ids=true | all-gather | bytes 1032192 | tf_op jit(solution)/shard_map/gather_dp/all_gather | solution.py:277
  135.6 0.1 copy.13
  135.7 0.8 copy.14.ids
  136.5 0.0 copy-done.2
  136.5 2.6 %sum_dp.1 = (f32[12,64,256]{2,1,0:T(8,128)}, bf16[32,96,128]{2,1,0:T(8,128)(2,1)}) custom-call(s32[1]{0:T(128)} %bitcast.5.core, s32[8,3]{1,0:T(8,128)} %copy.14.ids, bf16[8,224,256]{2,1,0:T(8,128)(2,1)} %bitcast.12), custom_call_target="tpu_custom_call" | custom-call | bytes 7500000 | tf_op jit(solution)/shard_map/sum_dp/pallas_call | solution.py:280
  139.1 6.1 %all-to-all-start.2 = ((bf16[32,96,128]{2,1,0:T(8,128)(2,1)}), bf16[32,96,128]{2,1,0:T(8,128)(2,1)S(1)}, u32[]{:S(2)}, u32[]{:S(2)}) async-start(bf16[32,96,128]{2,1,0:T(8,128)(2,1)} %get-tuple-element.25), calls=%async_computation.2 | async-start | bytes 1572864 | tf_op jit(solution)/shard_map/up_spread/all_to_all | solution.py:289
  145.3 5.1 %all-gather.3.cloned.1.call-done.weight = bf16[8192,1024]{1,0:T(8,128)(2,1)} async-done(((bf16[32,1024]{1,0:T(8,128)(2,1)}), bf16[8192,1024]{1,0:T(8,128)(2,1)}) %all-gather.3.cloned.1.call-update) | async-done | bytes 16777232 | tf_op jit(solution)/shard_map/frozen_gather/all_gather | solution.py:222
  150.4 12.9 %grad_input.1 = bf16[256,8192]{1,0:T(8,128)(2,1)} custom-call(bf16[256,1024]{1,0:T(8,128)(2,1)} %get-tuple-element.15.masked, bf16[8192,1024]{1,0:T(8,128)(2,1)} %all-gather.3.cloned.1.call-done.weight, bf16[256,192]{1,0:T(8,128)(2,1)} %get-tuple-element.16.back_slots, bf16[192,8192]{1,0:T(8,128)(2,1)} %copy-done.1), custom_call_target="tpu_custom_call" | custom-call | bytes 39000000 | tf_op jit(solution)/shard_map/grad_input/pallas_call | solution.py:292
  163.3 1.8 all-to-all-done.2.mine
  165.1 3.5 %collective-permute-start.15 = (bf16[32,96,128]{2,1,0:T(8,128)(2,1)S(1)}, bf16[32,96,128]{2,1,0:T(8,128)(2,1)S(1)}, u32[]{:S(2)}, u32[]{:S(2)}) collective-permute-start(bf16[32,96,128]{2,1,0:T(8,128)(2,1)S(1)} %all-to-all-done.2.mine), channel_id=1, source_target_pairs={{0,32},{32,0},{1,33},{33,1},{2,34},{34,2},{3,35},{35,3},{4,36},{36... | collective-permute-start | bytes 2359304 | tf_op jit(solution)/shard_map/up_swap/ppermute | solution.py:306
  168.6 1.9 %collective-permute-done.15.other = bf16[32,96,128]{2,1,0:T(8,128)(2,1)S(1)} collective-permute-done((bf16[32,96,128]{2,1,0:T(8,128)(2,1)S(1)}, bf16[32,96,128]{2,1,0:T(8,128)(2,1)S(1)}, u32[]{:S(2)}, u32[]{:S(2)}) %collective-permute-start.15) | collective-permute-done | bytes 786464 | tf_op jit(solution)/shard_map/up_swap/ppermute | solution.py:306
  170.5 0.9 copy-done.6
  171.4 3.2 %up_swap.1 = f32[12,64,1024]{2,1,0:T(8,128)} custom-call(s32[1]{0:T(128)} %bitcast.5.core, bf16[32,96,128]{2,1,0:T(8,128)(2,1)} %copy-done.3, bf16[32,96,128]{2,1,0:T(8,128)(2,1)} %copy-done.6), custom_call_target="tpu_custom_call" | custom-call | bytes 9000000 | tf_op jit(solution)/shard_map/up_swap/pallas_call | solution.py:307
  (31 shorter events, 0.3 us)
Async XLA Ops:
  7.2 1.0 copy-start
  7.2 143.2 %all-gather.3.cloned.1.call-start = ((), (), s32[]{:S(2)}) async-start(), calls=%async_computation.3 | async-start | bytes 16842752 | tf_op jit(solution)/shard_map/frozen_gather/all_gather | solution.py:222
  11.1 16.4 %collective-permute-start = (bf16[192,256]{1,0:T(8,128)(2,1)S(1)}, bf16[192,256]{1,0:T(8,128)(2,1)S(1)}, u32[]{:S(2)}, u32[]{:S(2)}) collective-permute-start(bf16[192,256]{1,0:T(8,128)(2,1)S(1)} %bitcast.13), channel_id=1, source_target_pairs={{0,1},{1,2},{2,3},{3,4},{4,5},{5,6},{6,7},{7,0},{8,9},{9,10},{10,1... | collective-permute-start | bytes 294920 | tf_op jit(solution)/shard_map/down_gather/ppermute | solution.py:24
  13.6 13.9 %collective-permute-start.1 = (bf16[192,256]{1,0:T(8,128)(2,1)S(1)}, bf16[192,256]{1,0:T(8,128)(2,1)S(1)}, u32[]{:S(2)}, u32[]{:S(2)}) collective-permute-start(bf16[192,256]{1,0:T(8,128)(2,1)S(1)} %bitcast.14), channel_id=1, source_target_pairs={{0,7},{1,0},{2,1},{3,2},{4,3},{5,4},{6,5},{7,6},{8,15},{9,8},{10,9... | collective-permute-start | bytes 294920 | tf_op jit(solution)/shard_map/down_gather/ppermute | solution.py:24
  23.2 19.0 %collective-permute-start.10 = (bf16[128,2176]{1,0:T(8,128)(2,1)}, bf16[128,2176]{1,0:T(8,128)(2,1)S(1)}, u32[]{:S(2)}, u32[]{:S(2)}) collective-permute-start(bf16[128,2176]{1,0:T(8,128)(2,1)} %get-tuple-element.20), channel_id=1, source_target_pairs={{0,24},{8,0},{16,8},{24,16},{1,25},{9,1},{17,9},{25,17},{2,26},{10... | collective-permute-start | bytes 1671176 | tf_op jit(solution)/shard_map/down_x/ppermute | solution.py:24
  25.6 16.5 %collective-permute-start.8 = (bf16[128,2176]{1,0:T(8,128)(2,1)}, bf16[128,2176]{1,0:T(8,128)(2,1)S(1)}, u32[]{:S(2)}, u32[]{:S(2)}) collective-permute-start(bf16[128,2176]{1,0:T(8,128)(2,1)} %get-tuple-element.18), channel_id=1, source_target_pairs={{0,8},{8,16},{16,24},{24,0},{1,9},{9,17},{17,25},{25,1},{2,10},{10... | collective-permute-start | bytes 1671176 | tf_op jit(solution)/shard_map/down_x/ppermute | solution.py:24
  25.7 26.1 %collective-permute-start.9 = (bf16[128,2176]{1,0:T(8,128)(2,1)}, bf16[128,2176]{1,0:T(8,128)(2,1)}, u32[]{:S(2)}, u32[]{:S(2)}) collective-permute-start(bf16[128,2176]{1,0:T(8,128)(2,1)} %get-tuple-element.19), channel_id=1, source_target_pairs={{0,16},{8,24},{16,0},{24,8},{1,17},{9,25},{17,1},{25,9},{2,18},{10... | collective-permute-start | bytes 1671176 | tf_op jit(solution)/shard_map/down_x/ppermute | solution.py:24
  27.5 5.1 %collective-permute-start.2 = (bf16[192,256]{1,0:T(8,128)(2,1)S(1)}, bf16[192,256]{1,0:T(8,128)(2,1)S(1)}, u32[]{:S(2)}, u32[]{:S(2)}) collective-permute-start(bf16[192,256]{1,0:T(8,128)(2,1)S(1)} %collective-permute-done), channel_id=1, source_target_pairs={{0,1},{1,2},{2,3},{3,4},{4,5},{5,6},{6,7},{7,0},{8,9},{9,10},{10,1... | collective-permute-start | bytes 294920 | tf_op jit(solution)/shard_map/down_gather/ppermute | solution.py:24
  27.6 5.0 %collective-permute-start.3 = (bf16[192,256]{1,0:T(8,128)(2,1)S(1)}, bf16[192,256]{1,0:T(8,128)(2,1)S(1)}, u32[]{:S(2)}, u32[]{:S(2)}) collective-permute-start(bf16[192,256]{1,0:T(8,128)(2,1)S(1)} %collective-permute-done.1), channel_id=1, source_target_pairs={{0,7},{1,0},{2,1},{3,2},{4,3},{5,4},{6,5},{7,6},{8,15},{9,8},{10,9... | collective-permute-start | bytes 294920 | tf_op jit(solution)/shard_map/down_gather/ppermute | solution.py:24
  32.6 5.0 %collective-permute-start.4 = (bf16[192,256]{1,0:T(8,128)(2,1)S(1)}, bf16[192,256]{1,0:T(8,128)(2,1)S(1)}, u32[]{:S(2)}, u32[]{:S(2)}) collective-permute-start(bf16[192,256]{1,0:T(8,128)(2,1)S(1)} %collective-permute-done.2), channel_id=1, source_target_pairs={{0,1},{1,2},{2,3},{3,4},{4,5},{5,6},{6,7},{7,0},{8,9},{9,10},{10,1... | collective-permute-start | bytes 294920 | tf_op jit(solution)/shard_map/down_gather/ppermute | solution.py:24
  32.6 5.0 %collective-permute-start.5 = (bf16[192,256]{1,0:T(8,128)(2,1)S(1)}, bf16[192,256]{1,0:T(8,128)(2,1)S(1)}, u32[]{:S(2)}, u32[]{:S(2)}) collective-permute-start(bf16[192,256]{1,0:T(8,128)(2,1)S(1)} %collective-permute-done.3), channel_id=1, source_target_pairs={{0,7},{1,0},{2,1},{3,2},{4,3},{5,4},{6,5},{7,6},{8,15},{9,8},{10,9... | collective-permute-start | bytes 294920 | tf_op jit(solution)/shard_map/down_gather/ppermute | solution.py:24
  37.6 4.5 %collective-permute-start.6 = (bf16[192,128]{1,0:T(8,128)(2,1)S(1)}, bf16[192,128]{1,0:T(8,128)(2,1)S(1)}, u32[]{:S(2)}, u32[]{:S(2)}) collective-permute-start(bf16[192,128]{1,0:T(8,128)(2,1)S(1)} %slice.22), channel_id=1, source_target_pairs={{0,1},{1,2},{2,3},{3,4},{4,5},{5,6},{6,7},{7,0},{8,9},{9,10},{10,1... | collective-permute-start | bytes 147464 | tf_op jit(solution)/shard_map/down_gather/ppermute | solution.py:24
  37.6 4.5 %collective-permute-start.7 = (bf16[192,128]{1,0:T(8,128)(2,1)S(1)}, bf16[192,128]{1,0:T(8,128)(2,1)S(1)}, u32[]{:S(2)}, u32[]{:S(2)}) collective-permute-start(bf16[192,128]{1,0:T(8,128)(2,1)S(1)} %slice.23), channel_id=1, source_target_pairs={{0,7},{1,0},{2,1},{3,2},{4,3},{5,4},{6,5},{7,6},{8,15},{9,8},{10,9... | collective-permute-start | bytes 147464 | tf_op jit(solution)/shard_map/down_gather/ppermute | solution.py:24
  42.1 12.3 %copy-start.7 = (bf16[128,2176]{1,0:T(8,128)(2,1)}, bf16[128,2176]{1,0:T(8,128)(2,1)S(1)}, u32[]{:S(2)}) copy-start(bf16[128,2176]{1,0:T(8,128)(2,1)S(1)} %collective-permute-done.10.refs_3_) | copy-start | bytes 1671172
  42.2 12.3 %copy-start.8 = (bf16[128,2176]{1,0:T(8,128)(2,1)}, bf16[128,2176]{1,0:T(8,128)(2,1)S(1)}, u32[]{:S(2)}) copy-start(bf16[128,2176]{1,0:T(8,128)(2,1)S(1)} %collective-permute-done.8.refs_1_) | copy-start | bytes 1671172
  51.8 17.3 %collective-permute-start.11 = (bf16[192,2048]{1,0:T(8,128)(2,1)S(1)}, bf16[192,2048]{1,0:T(8,128)(2,1)S(1)}, u32[]{:S(2)}, u32[]{:S(2)}) collective-permute-start(bf16[192,2048]{1,0:T(8,128)(2,1)S(1)} %constant_dynamic-update-slice_fusion.5), channel_id=1, source_target_pairs={{0,8},{8,16},{16,24},{24,0},{1,9},{9,17},{17,25},{25,1},{2,10},{10... | collective-permute-start | bytes 2359304 | tf_op jit(solution)/shard_map/down_gather/ppermute | solution.py:24
  51.8 17.4 %collective-permute-start.12 = (bf16[192,2048]{1,0:T(8,128)(2,1)S(1)}, bf16[192,2048]{1,0:T(8,128)(2,1)}, u32[]{:S(2)}, u32[]{:S(2)}) collective-permute-start(bf16[192,2048]{1,0:T(8,128)(2,1)S(1)} %constant_dynamic-update-slice_fusion.5), channel_id=1, source_target_pairs={{0,24},{8,0},{16,8},{24,16},{1,25},{9,1},{17,9},{25,17},{2,26},{10... | collective-permute-start | bytes 2359304 | tf_op jit(solution)/shard_map/down_gather/ppermute | solution.py:24
  58.3 32.8 %all-to-all-start = ((bf16[8,192,256]{2,1,0:T(8,128)(2,1)}), bf16[8,192,256]{2,1,0:T(8,128)(2,1)S(1)}, u32[]{:S(2)}, u32[]{:S(2)}) async-start(bf16[8,192,256]{2,1,0:T(8,128)(2,1)} %down_sum_x.1), calls=%async_computation | async-start | bytes 1572864 | tf_op jit(solution)/shard_map/down_z/all_to_all | solution.py:244
  69.1 13.2 %collective-permute-start.13 = (bf16[192,1024]{1,0:T(8,128)(2,1)S(1)}, bf16[192,1024]{1,0:T(8,128)(2,1)S(1)}, u32[]{:S(2)}, u32[]{:S(2)}) collective-permute-start(bf16[192,1024]{1,0:T(8,128)(2,1)S(1)} %slice.24), channel_id=1, source_target_pairs={{0,8},{8,16},{16,24},{24,0},{1,9},{9,17},{17,25},{25,1},{2,10},{10... | collective-permute-start | bytes 1179656 | tf_op jit(solution)/shard_map/down_gather/ppermute | solution.py:24
  70.3 12.1 %collective-permute-start.14 = (bf16[192,1024]{1,0:T(8,128)(2,1)S(1)}, bf16[192,1024]{1,0:T(8,128)(2,1)S(1)}, u32[]{:S(2)}, u32[]{:S(2)}) collective-permute-start(bf16[192,1024]{1,0:T(8,128)(2,1)S(1)} %slice.25), channel_id=1, source_target_pairs={{0,24},{8,0},{16,8},{24,16},{1,25},{9,1},{17,9},{25,17},{2,26},{10... | collective-permute-start | bytes 1179656 | tf_op jit(solution)/shard_map/down_gather/ppermute | solution.py:24
  82.4 1.7 copy-start.1
  91.1 7.0 %copy-start.4 = (bf16[8,192,256]{2,1,0:T(8,128)(2,1)}, bf16[8,192,256]{2,1,0:T(8,128)(2,1)S(1)}, u32[]{:S(2)}) copy-start(bf16[8,192,256]{2,1,0:T(8,128)(2,1)S(1)} %all-to-all-done.parts) | copy-start | bytes 2359300
  91.1 18.4 %all-to-all-start.1 = ((bf16[32,64,128]{2,1,0:T(8,128)(2,1)}), bf16[32,64,128]{2,1,0:T(8,128)(2,1)S(1)}, u32[]{:S(2)}, u32[]{:S(2)}) async-start(bf16[32,64,128]{2,1,0:T(8,128)(2,1)} %up_terms.1), calls=%async_computation.1 | async-start | bytes 1048576 | tf_op jit(solution)/shard_map/up_tensor/all_to_all | solution.py:267
  109.4 0.8 copy-start.5
  135.6 0.9 copy-start.2
  139.1 26.0 %all-to-all-start.2 = ((bf16[32,96,128]{2,1,0:T(8,128)(2,1)}), bf16[32,96,128]{2,1,0:T(8,128)(2,1)S(1)}, u32[]{:S(2)}, u32[]{:S(2)}) async-start(bf16[32,96,128]{2,1,0:T(8,128)(2,1)} %get-tuple-element.25), calls=%async_computation.2 | async-start | bytes 1572864 | tf_op jit(solution)/shard_map/up_spread/all_to_all | solution.py:289
  165.1 5.4 %copy-start.3 = (bf16[32,96,128]{2,1,0:T(8,128)(2,1)}, bf16[32,96,128]{2,1,0:T(8,128)(2,1)S(1)}, u32[]{:S(2)}) copy-start(bf16[32,96,128]{2,1,0:T(8,128)(2,1)S(1)} %all-to-all-done.2.mine) | copy-start | bytes 2359300
  165.1 5.4 %collective-permute-start.15 = (bf16[32,96,128]{2,1,0:T(8,128)(2,1)S(1)}, bf16[32,96,128]{2,1,0:T(8,128)(2,1)S(1)}, u32[]{:S(2)}, u32[]{:S(2)}) collective-permute-start(bf16[32,96,128]{2,1,0:T(8,128)(2,1)S(1)} %all-to-all-done.2.mine), channel_id=1, source_target_pairs={{0,32},{32,0},{1,33},{33,1},{2,34},{34,2},{3,35},{35,3},{4,36},{36... | collective-permute-start | bytes 2359304 | tf_op jit(solution)/shard_map/up_swap/ppermute | solution.py:306
  170.5 0.9 copy-start.6
Sparse Core Ops, SparseCore 0:
  11.7 138.6 all-gather.2

commit v3 on v2

--- a/solution.py
+++ b/solution.py
@@ -91,7 +91,7 @@
     tiles = slots.shape[0]
     tile_rows = act.shape[0] // tiles
     lanes = out.shape[2]
-    deep = out.shape[1] // tiles - 16
+    deep = out.shape[1] // tiles - 8
     rank = NX * deep
     terms, marks = [], []
     for tile in range(tiles):
@@ -100,14 +100,14 @@
         low = nt(act[rows, :], down[mine, :]).astype(BF16)
         twice = low * jnp.asarray(ADAPTER_SCALING, BF16)
         terms.append(tn(twice, masked[rows, :]).astype(BF16))
-        marks.append(jnp.full((16, lanes), slots[tile].astype(F32), F32).astype(BF16))
+        marks.append(jnp.full((8, lanes), slots[tile].astype(F32), F32))
+    marks = jnp.concatenate(marks, axis=0).astype(BF16)
     for to_x in range(NX):
         for to_z in range(NZ):
             for tile in range(tiles):
                 cut = terms[tile][to_x * deep : (to_x + 1) * deep, to_z * lanes : (to_z + 1) * lanes]
                 out[to_x * NZ + to_z, tile * deep : (tile + 1) * deep, :] = cut
-                first = tiles * deep + tile * 16
-                out[to_x * NZ + to_z, first : first + 16, :] = marks[tile]
+            out[to_x * NZ + to_z, tiles * deep :, :] = marks
 
 
 def up_sum_kernel(tiles, deep, held, downs, parts, out):
@@ -119,9 +119,9 @@
         total = jnp.zeros((deep, lanes), F32)
         for source in range(parts.shape[0]):
             for tile in range(tiles):
-                mark = parts[source, tiles * deep + tile * 16 : tiles * deep + (tile + 1) * 16, :].astype(F32)
+                mark = parts[source, tiles * deep :, :].astype(F32)[tile * 8 : (tile + 1) * 8]
                 part = parts[source, tile * deep : (tile + 1) * deep, :].astype(F32)
-                total = total + jnp.where(mark[:deep] == slot, part, 0.0)
+                total = total + jnp.where(jnp.concatenate([mark] * (deep // 8), axis=0) == slot, part, 0.0)
         sums.append(total)
     sums = jnp.concatenate(sums, axis=0)
     half = sums.shape[0] // 2
@@ -258,7 +258,7 @@
     with jax.named_scope("up_terms"):
         up_terms = pl.pallas_call(
             low_kernel,
-            out_shape=shape((NX * NZ, tiles * (deep + 16), lanes), BF16),
+            out_shape=shape((NX * NZ, tiles * (deep + 8), lanes), BF16),
             in_specs=[SMEM] + [VMEM] * 3,
             out_specs=VMEM,
             compiler_params=BIG, cost_estimate=cost(7),
@@ -288,7 +288,7 @@
     with jax.named_scope("up_spread"):
         square = lax.all_to_all(up_copies, ("x", "z"), 0, 0)
     with jax.named_scope("grad_input"):
-        block = 1024
+        block = 2048
         grad_input = pl.pallas_call(
             input_kernel,
             grid=(width // block,),

time: 182 us -> 183 us (level)
  waiting for transfers between devices: 47.7 us -> 53.9 us
  starting transfers between devices: 46 us -> 41.1 us
    all_gather x1, waiting for transfers between devices: 5.15 us -> 14.1 us  [body(): lax.all_gather(own_part, ('x', 'z', 'y', 'core'), axis=0, tiled=True)]
    ppermute x1, starting transfers between devices: 3.47 us -> 0.49 us  [body(): sibling = lax.ppermute(after(square, grad_input), 'core', SWAP)]
    all_to_all x1, starting transfers between devices: 6.14 us -> 4.23 us  [body(): square = lax.all_to_all(up_copies, ('x', 'z'), 0, 0)]
  transfers between devices with their start and end apart: 20 -> 20, of which waited for: 10 -> 9; matrix products, arithmetic and copies ran while one was open for 3% -> 3% of each run, Pallas kernels for 20% -> 19%
where the time goes in v3:
time: 183 us; the launch traced here: 181 us
  waiting for transfers between devices  53.9 us (29%)
  starting transfers between devices  41.1 us (22%)
  Pallas kernels  37.4 us (20%)
  blocking collectives  23.2 us (13%)
  between operations  14.3 us (8%)
  local copies, waits for them, and re-layouts  10.5 us (6%)
    ppermute x15, waiting for transfers between devices, shift(): lax.ppermute(value, axis, [(i, (i + by) % size) for i in range(size)])  29.3 us
    ppermute x15, starting transfers between devices, shift(): lax.ppermute(value, axis, [(i, (i + by) % size) for i in range(size)])  24.5 us
    all_gather x1, blocking collectives, body(): groups = lax.all_gather(packed, ('y', 'core'), axis=0, tiled=False)  23.2 us
    all_gather x1, waiting for transfers between devices, body(): lax.all_gather(own_part, ('x', 'z', 'y', 'core'), axis=0, tiled=True)  14.1 us
    pallas_call x1, Pallas kernels, body(): pl.pallas_call(input_kernel, grid=(width // block,), out_shape=shape((row...  11.4 us
    all_to_all x1, waiting for transfers between devices, body(): up_got = lax.all_to_all(up_terms, ('x', 'z'), 0, 0, tiled=True)  8.45 us
    all_to_all x1, starting transfers between devices, body(): up_got = lax.all_to_all(up_terms, ('x', 'z'), 0, 0, tiled=True)  6.97 us
    pallas_call x1, Pallas kernels, body(): pl.pallas_call(low_kernel, out_shape=shape((NX * NZ, tiles * (deep + 8),...  6.92 us
  transfers between devices with their start and end apart: 20, of which 9 were waited for; matrix products, arithmetic and copies ran while one was open for 3% of the time, Pallas kernels for 19%

profile of v3, /device:TPU:1, one launch (start us, length us, event | category | flops | bytes accessed | tf_op | source)
XLA Modules:
  0.0 181.0 jit_solution(2323371225370748398)
XLA Ops:
  7.2 0.0 copy-start
  7.2 0.0 all-gather.3.cloned.1.call-start
  7.2 1.0 copy-done
  8.2 0.6 constant_dynamic-slice_fusion
  8.8 0.0 all-gather.3.cloned.1.call-update
  8.9 0.7 fusion
  9.5 1.5 gather_fusion
  11.1 2.5 %collective-permute-start = (bf16[192,256]{1,0:T(8,128)(2,1)S(1)}, bf16[192,256]{1,0:T(8,128)(2,1)S(1)}, u32[]{:S(2)}, u32[]{:S(2)}) collective-permute-start(bf16[192,256]{1,0:T(8,128)(2,1)S(1)} %bitcast.13), channel_id=1, source_target_pairs={{0,1},{1,2},{2,3},{3,4},{4,5},{5,6},{6,7},{7,0},{8,9},{9,10},{10,1... | collective-permute-start | bytes 294920 | tf_op jit(solution)/shard_map/down_gather/ppermute | solution.py:24
  13.6 4.0 %collective-permute-start.1 = (bf16[192,256]{1,0:T(8,128)(2,1)S(1)}, bf16[192,256]{1,0:T(8,128)(2,1)S(1)}, u32[]{:S(2)}, u32[]{:S(2)}) collective-permute-start(bf16[192,256]{1,0:T(8,128)(2,1)S(1)} %bitcast.14), channel_id=1, source_target_pairs={{0,7},{1,0},{2,1},{3,2},{4,3},{5,4},{6,5},{7,6},{8,15},{9,8},{10,9... | collective-permute-start | bytes 294920 | tf_op jit(solution)/shard_map/down_gather/ppermute | solution.py:24
  17.7 5.5 %down_terms.1 = (bf16[256,1024]{1,0:T(8,128)(2,1)}, bf16[256,192]{1,0:T(8,128)(2,1)}, bf16[128,2176]{1,0:T(8,128)(2,1)}, bf16[128,2176]{1,0:T(8,128)(2,1)}, bf16...) custom-call(s32[1]{0:T(128)} %bitcast.x, s32[1,3]{1,0:T(1,128)} %held.3, s32[2]{0:T(128)} %slots.3, s32[2]{0:T(128)} %lengths.1, ...), custom_call_target="tpu_custom_call" | custom-call | bytes 16500000 | tf_op jit(solution)/shard_map/down_terms/pallas_call | solution.py:225
  23.2 2.5 %collective-permute-start.10 = (bf16[128,2176]{1,0:T(8,128)(2,1)}, bf16[128,2176]{1,0:T(8,128)(2,1)S(1)}, u32[]{:S(2)}, u32[]{:S(2)}) collective-permute-start(bf16[128,2176]{1,0:T(8,128)(2,1)} %get-tuple-element.20), channel_id=1, source_target_pairs={{0,24},{8,0},{16,8},{24,16},{1,25},{9,1},{17,9},{25,17},{2,26},{10... | collective-permute-start | bytes 1671176 | tf_op jit(solution)/shard_map/down_x/ppermute | solution.py:24
  25.6 0.0 collective-permute-start.8
  25.7 1.7 collective-permute-start.9
  27.4 0.1 broadcast_in_dim.8
  27.5 0.0 collective-permute-done
  27.5 0.0 collective-permute-done.1
  27.5 0.1 collective-permute-start.2
  27.6 2.7 %collective-permute-start.3 = (bf16[192,256]{1,0:T(8,128)(2,1)S(1)}, bf16[192,256]{1,0:T(8,128)(2,1)S(1)}, u32[]{:S(2)}, u32[]{:S(2)}) collective-permute-start(bf16[192,256]{1,0:T(8,128)(2,1)S(1)} %collective-permute-done.1), channel_id=1, source_target_pairs={{0,7},{1,0},{2,1},{3,2},{4,3},{5,4},{6,5},{7,6},{8,15},{9,8},{10,9... | collective-permute-start | bytes 294920 | tf_op jit(solution)/shard_map/down_gather/ppermute | solution.py:24
  30.3 2.3 %collective-permute-done.2 = bf16[192,256]{1,0:T(8,128)(2,1)S(1)} collective-permute-done((bf16[192,256]{1,0:T(8,128)(2,1)S(1)}, bf16[192,256]{1,0:T(8,128)(2,1)S(1)}, u32[]{:S(2)}, u32[]{:S(2)}) %collective-permute-start.2) | collective-permute-done | bytes 98336 | tf_op jit(solution)/shard_map/down_gather/ppermute | solution.py:24
  32.6 0.0 collective-permute-start.4
  32.6 0.0 collective-permute-done.3
  32.6 2.7 %collective-permute-start.5 = (bf16[192,256]{1,0:T(8,128)(2,1)S(1)}, bf16[192,256]{1,0:T(8,128)(2,1)S(1)}, u32[]{:S(2)}, u32[]{:S(2)}) collective-permute-start(bf16[192,256]{1,0:T(8,128)(2,1)S(1)} %collective-permute-done.3), channel_id=1, source_target_pairs={{0,7},{1,0},{2,1},{3,2},{4,3},{5,4},{6,5},{7,6},{8,15},{9,8},{10,9... | collective-permute-start | bytes 294920 | tf_op jit(solution)/shard_map/down_gather/ppermute | solution.py:24
  35.3 2.3 %collective-permute-done.4 = bf16[192,256]{1,0:T(8,128)(2,1)S(1)} collective-permute-done((bf16[192,256]{1,0:T(8,128)(2,1)S(1)}, bf16[192,256]{1,0:T(8,128)(2,1)S(1)}, u32[]{:S(2)}, u32[]{:S(2)}) %collective-permute-start.4) | collective-permute-done | bytes 98336 | tf_op jit(solution)/shard_map/down_gather/ppermute | solution.py:24
  37.6 0.0 collective-permute-start.6
  37.6 0.0 collective-permute-done.5
  37.6 2.7 %collective-permute-start.7 = (bf16[192,128]{1,0:T(8,128)(2,1)S(1)}, bf16[192,128]{1,0:T(8,128)(2,1)S(1)}, u32[]{:S(2)}, u32[]{:S(2)}) collective-permute-start(bf16[192,128]{1,0:T(8,128)(2,1)S(1)} %slice.23), channel_id=1, source_target_pairs={{0,7},{1,0},{2,1},{3,2},{4,3},{5,4},{6,5},{7,6},{8,15},{9,8},{10,9... | collective-permute-start | bytes 147464 | tf_op jit(solution)/shard_map/down_gather/ppermute | solution.py:24
  40.4 1.7 collective-permute-done.6
  42.1 0.0 collective-permute-done.7
  42.1 0.0 collective-permute-done.10.refs_3_
  42.2 9.6 %collective-permute-done.9.refs_2_ = bf16[128,2176]{1,0:T(8,128)(2,1)} collective-permute-done((bf16[128,2176]{1,0:T(8,128)(2,1)}, bf16[128,2176]{1,0:T(8,128)(2,1)}, u32[]{:S(2)}, u32[]{:S(2)}) %collective-permute-start.9) | collective-permute-done | bytes 557088 | tf_op jit(solution)/shard_map/down_x/ppermute | solution.py:24
  51.8 2.7 %collective-permute-start.12 = (bf16[192,2048]{1,0:T(8,128)(2,1)S(1)}, bf16[192,2048]{1,0:T(8,128)(2,1)}, u32[]{:S(2)}, u32[]{:S(2)}) collective-permute-start(bf16[192,2048]{1,0:T(8,128)(2,1)S(1)} %constant_dynamic-update-slice_fusion.5), channel_id=1, source_target_pairs={{0,24},{8,0},{16,8},{24,16},{1,25},{9,1},{17,9},{25,17},{2,26},{10... | collective-permute-start | bytes 2359304 | tf_op jit(solution)/shard_map/down_gather/ppermute | solution.py:24
  54.5 3.8 %down_sum_x.1 = bf16[8,192,256]{2,1,0:T(8,128)(2,1)} custom-call(bf16[128,2176]{1,0:T(8,128)(2,1)} %get-tuple-element.17.refs_0_, bf16[128,2176]{1,0:T(8,128)(2,1)} %copy-done.8, bf16[128,2176]{1,0:T(8,128)(2,1)} %collective-permute-done.9.refs_2_, bf16[128,2176]{1,0:T(8,128)(2,1)} %copy-done.7), custom_call_target="tpu_custom_call" | custom-call | bytes 12000000 | tf_op jit(solution)/shard_map/down_sum_x/pallas_call | solution.py:236
  58.3 4.9 %all-to-all-start = ((bf16[8,192,256]{2,1,0:T(8,128)(2,1)}), bf16[8,192,256]{2,1,0:T(8,128)(2,1)S(1)}, u32[]{:S(2)}, u32[]{:S(2)}) async-start(bf16[8,192,256]{2,1,0:T(8,128)(2,1)} %down_sum_x.1), calls=%async_computation | async-start | bytes 1572864 | tf_op jit(solution)/shard_map/down_z/all_to_all | solution.py:244
  63.2 0.3 broadcast_in_dim.7
  63.6 0.1 constant_dynamic-update-slice_fusion.4
  63.6 5.4 %collective-permute-done.11 = bf16[192,2048]{1,0:T(8,128)(2,1)S(1)} collective-permute-done((bf16[192,2048]{1,0:T(8,128)(2,1)S(1)}, bf16[192,2048]{1,0:T(8,128)(2,1)S(1)}, u32[]{:S(2)}, u32[]{:S(2)}) %collective-permute-start.11) | collective-permute-done | bytes 786464 | tf_op jit(solution)/shard_map/down_gather/ppermute | solution.py:24
  69.1 0.1 collective-permute-start.13
  69.2 1.1 slice.25
  70.3 2.7 %collective-permute-start.14 = (bf16[192,1024]{1,0:T(8,128)(2,1)S(1)}, bf16[192,1024]{1,0:T(8,128)(2,1)S(1)}, u32[]{:S(2)}, u32[]{:S(2)}) collective-permute-start(bf16[192,1024]{1,0:T(8,128)(2,1)S(1)} %slice.25), channel_id=1, source_target_pairs={{0,24},{8,0},{16,8},{24,16},{1,25},{9,1},{17,9},{25,17},{2,26},{10... | collective-permute-start | bytes 1179656 | tf_op jit(solution)/shard_map/down_gather/ppermute | solution.py:24
  73.0 0.1 constant_dynamic-update-slice_fusion.3
  73.1 1.2 constant_dynamic-update-slice_fusion.2
  74.3 8.0 %collective-permute-done.13 = bf16[192,1024]{1,0:T(8,128)(2,1)S(1)} collective-permute-done((bf16[192,1024]{1,0:T(8,128)(2,1)S(1)}, bf16[192,1024]{1,0:T(8,128)(2,1)S(1)}, u32[]{:S(2)}, u32[]{:S(2)}) %collective-permute-start.13) | collective-permute-done | bytes 393248 | tf_op jit(solution)/shard_map/down_gather/ppermute | solution.py:24
  82.4 0.0 collective-permute-done.14
  82.4 0.0 copy-start.1
  82.5 1.7 copy-done.1
  84.1 6.9 %up_terms.1 = bf16[32,48,128]{2,1,0:T(8,128)(2,1)} custom-call(s32[2]{0:T(128)} %slots.3, bf16[256,8192]{1,0:T(8,128)(2,1)} %act.3, bf16[256,1024]{1,0:T(8,128)(2,1)} %get-tuple-element.15.masked, bf16[192,8192]{1,0:T(8,128)(2,1)} %copy-done.1), custom_call_target="tpu_custom_call" | custom-call | bytes 21000000 | tf_op jit(solution)/shard_map/up_terms/pallas_call | solution.py:259
  91.0 0.0 all-to-all-done.parts
  91.0 7.0 %all-to-all-start.1 = ((bf16[32,48,128]{2,1,0:T(8,128)(2,1)}), bf16[32,48,128]{2,1,0:T(8,128)(2,1)S(1)}, u32[]{:S(2)}, u32[]{:S(2)}) async-start(bf16[32,48,128]{2,1,0:T(8,128)(2,1)} %up_terms.1), calls=%async_computation.1 | async-start | bytes 786432 | tf_op jit(solution)/shard_map/up_tensor/all_to_all | solution.py:267
  98.0 1.9 %down_sum_z.1.downs = bf16[192,256]{1,0:T(8,128)(2,1)} custom-call(bf16[8,192,256]{2,1,0:T(8,128)(2,1)} %copy-done.4), custom_call_target="tpu_custom_call" | custom-call | bytes 6000000 | tf_op jit(solution)/shard_map/down_sum_z/pallas_call | solution.py:246
  99.9 8.5 %all-to-all-done.1.parts = bf16[32,48,128]{2,1,0:T(8,128)(2,1)S(1)} async-done(((bf16[32,48,128]{2,1,0:T(8,128)(2,1)}), bf16[32,48,128]{2,1,0:T(8,128)(2,1)S(1)}, u32[]{:S(2)}, u32[]{:S(2)}) %all-to-all-start.1) | async-done | bytes 393248 | tf_op jit(solution)/shard_map/up_tensor/all_to_all | solution.py:267
  108.4 0.7 copy-done.5
  109.1 2.1 %up_sum.1 = bf16[224,256]{1,0:T(8,128)(2,1)} custom-call(s32[1,3]{1,0:T(1,128)} %held.3, bf16[192,256]{1,0:T(8,128)(2,1)} %down_sum_z.1.downs, bf16[32,48,128]{2,1,0:T(8,128)(2,1)} %copy-done.5), custom_call_target="tpu_custom_call" | custom-call | bytes 6000000 | tf_op jit(solution)/shard_map/up_sum/pallas_call | solution.py:269
  111.2 23.2 %all-gather = bf16[1792,256]{1,0:T(8,128)(2,1)S(1)} all-gather(bf16[224,256]{1,0:T(8,128)(2,1)} %up_sum.1), channel_id=2, replica_groups=mesh['y'=4,'core'=2,'x'=4,'z'=8] {'y','core'}, dimensions={0}, use_global_device_ids=true | all-gather | bytes 1032192 | tf_op jit(solution)/shard_map/gather_dp/all_gather | solution.py:277
  134.4 0.1 copy.13
  134.5 0.8 copy.14.ids
  135.3 0.0 copy-done.2
  135.3 2.6 %sum_dp.1 = (f32[12,64,256]{2,1,0:T(8,128)}, bf16[32,96,128]{2,1,0:T(8,128)(2,1)}) custom-call(s32[1]{0:T(128)} %bitcast.5.core, s32[8,3]{1,0:T(8,128)} %copy.14.ids, bf16[8,224,256]{2,1,0:T(8,128)(2,1)} %bitcast.12), custom_call_target="tpu_custom_call" | custom-call | bytes 7500000 | tf_op jit(solution)/shard_map/sum_dp/pallas_call | solution.py:280
  137.9 4.2 %all-to-all-start.2 = ((bf16[32,96,128]{2,1,0:T(8,128)(2,1)}), bf16[32,96,128]{2,1,0:T(8,128)(2,1)S(1)}, u32[]{:S(2)}, u32[]{:S(2)}) async-start(bf16[32,96,128]{2,1,0:T(8,128)(2,1)} %get-tuple-element.25), calls=%async_computation.2 | async-start | bytes 1572864 | tf_op jit(solution)/shard_map/up_spread/all_to_all | solution.py:289
  142.1 14.1 %all-gather.3.cloned.1.call-done.weight = bf16[8192,1024]{1,0:T(8,128)(2,1)} async-done(((bf16[32,1024]{1,0:T(8,128)(2,1)}), bf16[8192,1024]{1,0:T(8,128)(2,1)}) %all-gather.3.cloned.1.call-update) | async-done | bytes 16777232 | tf_op jit(solution)/shard_map/frozen_gather/all_gather | solution.py:222
  156.3 11.4 %grad_input.1 = bf16[256,8192]{1,0:T(8,128)(2,1)} custom-call(bf16[256,1024]{1,0:T(8,128)(2,1)} %get-tuple-element.15.masked, bf16[8192,1024]{1,0:T(8,128)(2,1)} %all-gather.3.cloned.1.call-done.weight, bf16[256,192]{1,0:T(8,128)(2,1)} %get-tuple-element.16.back_slots, bf16[192,8192]{1,0:T(8,128)(2,1)} %copy-done.1), custom_call_target="tpu_custom_call" | custom-call | bytes 39000000 | tf_op jit(solution)/shard_map/grad_input/pallas_call | solution.py:292
  167.6 0.5 collective-permute-start.15
  168.1 1.9 %collective-permute-done.15.other = bf16[32,96,128]{2,1,0:T(8,128)(2,1)S(1)} collective-permute-done((bf16[32,96,128]{2,1,0:T(8,128)(2,1)S(1)}, bf16[32,96,128]{2,1,0:T(8,128)(2,1)S(1)}, u32[]{:S(2)}, u32[]{:S(2)}) %collective-permute-start.15) | collective-permute-done | bytes 786464 | tf_op jit(solution)/shard_map/up_swap/ppermute | solution.py:306
  170.0 0.9 copy-done.6
  170.9 3.2 %up_swap.1 = f32[12,64,1024]{2,1,0:T(8,128)} custom-call(s32[1]{0:T(128)} %bitcast.5.core, bf16[32,96,128]{2,1,0:T(8,128)(2,1)} %copy-done.3, bf16[32,96,128]{2,1,0:T(8,128)(2,1)} %copy-done.6), custom_call_target="tpu_custom_call" | custom-call | bytes 9000000 | tf_op jit(solution)/shard_map/up_swap/pallas_call | solution.py:307
  (31 shorter events, 0.3 us)
Async XLA Ops:
  7.2 1.0 copy-start
  7.2 149.1 %all-gather.3.cloned.1.call-start = ((), (), s32[]{:S(2)}) async-start(), calls=%async_computation.3 | async-start | bytes 16842752 | tf_op jit(solution)/shard_map/frozen_gather/all_gather | solution.py:222
  11.1 16.4 %collective-permute-start = (bf16[192,256]{1,0:T(8,128)(2,1)S(1)}, bf16[192,256]{1,0:T(8,128)(2,1)S(1)}, u32[]{:S(2)}, u32[]{:S(2)}) collective-permute-start(bf16[192,256]{1,0:T(8,128)(2,1)S(1)} %bitcast.13), channel_id=1, source_target_pairs={{0,1},{1,2},{2,3},{3,4},{4,5},{5,6},{6,7},{7,0},{8,9},{9,10},{10,1... | collective-permute-start | bytes 294920 | tf_op jit(solution)/shard_map/down_gather/ppermute | solution.py:24
  13.6 13.9 %collective-permute-start.1 = (bf16[192,256]{1,0:T(8,128)(2,1)S(1)}, bf16[192,256]{1,0:T(8,128)(2,1)S(1)}, u32[]{:S(2)}, u32[]{:S(2)}) collective-permute-start(bf16[192,256]{1,0:T(8,128)(2,1)S(1)} %bitcast.14), channel_id=1, source_target_pairs={{0,7},{1,0},{2,1},{3,2},{4,3},{5,4},{6,5},{7,6},{8,15},{9,8},{10,9... | collective-permute-start | bytes 294920 | tf_op jit(solution)/shard_map/down_gather/ppermute | solution.py:24
  23.2 19.0 %collective-permute-start.10 = (bf16[128,2176]{1,0:T(8,128)(2,1)}, bf16[128,2176]{1,0:T(8,128)(2,1)S(1)}, u32[]{:S(2)}, u32[]{:S(2)}) collective-permute-start(bf16[128,2176]{1,0:T(8,128)(2,1)} %get-tuple-element.20), channel_id=1, source_target_pairs={{0,24},{8,0},{16,8},{24,16},{1,25},{9,1},{17,9},{25,17},{2,26},{10... | collective-permute-start | bytes 1671176 | tf_op jit(solution)/shard_map/down_x/ppermute | solution.py:24
  25.6 16.5 %collective-permute-start.8 = (bf16[128,2176]{1,0:T(8,128)(2,1)}, bf16[128,2176]{1,0:T(8,128)(2,1)S(1)}, u32[]{:S(2)}, u32[]{:S(2)}) collective-permute-start(bf16[128,2176]{1,0:T(8,128)(2,1)} %get-tuple-element.18), channel_id=1, source_target_pairs={{0,8},{8,16},{16,24},{24,0},{1,9},{9,17},{17,25},{25,1},{2,10},{10... | collective-permute-start | bytes 1671176 | tf_op jit(solution)/shard_map/down_x/ppermute | solution.py:24
  25.7 26.1 %collective-permute-start.9 = (bf16[128,2176]{1,0:T(8,128)(2,1)}, bf16[128,2176]{1,0:T(8,128)(2,1)}, u32[]{:S(2)}, u32[]{:S(2)}) collective-permute-start(bf16[128,2176]{1,0:T(8,128)(2,1)} %get-tuple-element.19), channel_id=1, source_target_pairs={{0,16},{8,24},{16,0},{24,8},{1,17},{9,25},{17,1},{25,9},{2,18},{10... | collective-permute-start | bytes 1671176 | tf_op jit(solution)/shard_map/down_x/ppermute | solution.py:24
  27.5 5.1 %collective-permute-start.2 = (bf16[192,256]{1,0:T(8,128)(2,1)S(1)}, bf16[192,256]{1,0:T(8,128)(2,1)S(1)}, u32[]{:S(2)}, u32[]{:S(2)}) collective-permute-start(bf16[192,256]{1,0:T(8,128)(2,1)S(1)} %collective-permute-done), channel_id=1, source_target_pairs={{0,1},{1,2},{2,3},{3,4},{4,5},{5,6},{6,7},{7,0},{8,9},{9,10},{10,1... | collective-permute-start | bytes 294920 | tf_op jit(solution)/shard_map/down_gather/ppermute | solution.py:24
  27.6 5.0 %collective-permute-start.3 = (bf16[192,256]{1,0:T(8,128)(2,1)S(1)}, bf16[192,256]{1,0:T(8,128)(2,1)S(1)}, u32[]{:S(2)}, u32[]{:S(2)}) collective-permute-start(bf16[192,256]{1,0:T(8,128)(2,1)S(1)} %collective-permute-done.1), channel_id=1, source_target_pairs={{0,7},{1,0},{2,1},{3,2},{4,3},{5,4},{6,5},{7,6},{8,15},{9,8},{10,9... | collective-permute-start | bytes 294920 | tf_op jit(solution)/shard_map/down_gather/ppermute | solution.py:24
  32.6 5.0 %collective-permute-start.4 = (bf16[192,256]{1,0:T(8,128)(2,1)S(1)}, bf16[192,256]{1,0:T(8,128)(2,1)S(1)}, u32[]{:S(2)}, u32[]{:S(2)}) collective-permute-start(bf16[192,256]{1,0:T(8,128)(2,1)S(1)} %collective-permute-done.2), channel_id=1, source_target_pairs={{0,1},{1,2},{2,3},{3,4},{4,5},{5,6},{6,7},{7,0},{8,9},{9,10},{10,1... | collective-permute-start | bytes 294920 | tf_op jit(solution)/shard_map/down_gather/ppermute | solution.py:24
  32.6 5.0 %collective-permute-start.5 = (bf16[192,256]{1,0:T(8,128)(2,1)S(1)}, bf16[192,256]{1,0:T(8,128)(2,1)S(1)}, u32[]{:S(2)}, u32[]{:S(2)}) collective-permute-start(bf16[192,256]{1,0:T(8,128)(2,1)S(1)} %collective-permute-done.3), channel_id=1, source_target_pairs={{0,7},{1,0},{2,1},{3,2},{4,3},{5,4},{6,5},{7,6},{8,15},{9,8},{10,9... | collective-permute-start | bytes 294920 | tf_op jit(solution)/shard_map/down_gather/ppermute | solution.py:24
  37.6 4.5 %collective-permute-start.6 = (bf16[192,128]{1,0:T(8,128)(2,1)S(1)}, bf16[192,128]{1,0:T(8,128)(2,1)S(1)}, u32[]{:S(2)}, u32[]{:S(2)}) collective-permute-start(bf16[192,128]{1,0:T(8,128)(2,1)S(1)} %slice.22), channel_id=1, source_target_pairs={{0,1},{1,2},{2,3},{3,4},{4,5},{5,6},{6,7},{7,0},{8,9},{9,10},{10,1... | collective-permute-start | bytes 147464 | tf_op jit(solution)/shard_map/down_gather/ppermute | solution.py:24
  37.6 4.5 %collective-permute-start.7 = (bf16[192,128]{1,0:T(8,128)(2,1)S(1)}, bf16[192,128]{1,0:T(8,128)(2,1)S(1)}, u32[]{:S(2)}, u32[]{:S(2)}) collective-permute-start(bf16[192,128]{1,0:T(8,128)(2,1)S(1)} %slice.23), channel_id=1, source_target_pairs={{0,7},{1,0},{2,1},{3,2},{4,3},{5,4},{6,5},{7,6},{8,15},{9,8},{10,9... | collective-permute-start | bytes 147464 | tf_op jit(solution)/shard_map/down_gather/ppermute | solution.py:24
  42.1 12.3 %copy-start.7 = (bf16[128,2176]{1,0:T(8,128)(2,1)}, bf16[128,2176]{1,0:T(8,128)(2,1)S(1)}, u32[]{:S(2)}) copy-start(bf16[128,2176]{1,0:T(8,128)(2,1)S(1)} %collective-permute-done.10.refs_3_) | copy-start | bytes 1671172
  42.2 12.3 %copy-start.8 = (bf16[128,2176]{1,0:T(8,128)(2,1)}, bf16[128,2176]{1,0:T(8,128)(2,1)S(1)}, u32[]{:S(2)}) copy-start(bf16[128,2176]{1,0:T(8,128)(2,1)S(1)} %collective-permute-done.8.refs_1_) | copy-start | bytes 1671172
  51.8 17.3 %collective-permute-start.11 = (bf16[192,2048]{1,0:T(8,128)(2,1)S(1)}, bf16[192,2048]{1,0:T(8,128)(2,1)S(1)}, u32[]{:S(2)}, u32[]{:S(2)}) collective-permute-start(bf16[192,2048]{1,0:T(8,128)(2,1)S(1)} %constant_dynamic-update-slice_fusion.5), channel_id=1, source_target_pairs={{0,8},{8,16},{16,24},{24,0},{1,9},{9,17},{17,25},{25,1},{2,10},{10... | collective-permute-start | bytes 2359304 | tf_op jit(solution)/shard_map/down_gather/ppermute | solution.py:24
  51.8 17.4 %collective-permute-start.12 = (bf16[192,2048]{1,0:T(8,128)(2,1)S(1)}, bf16[192,2048]{1,0:T(8,128)(2,1)}, u32[]{:S(2)}, u32[]{:S(2)}) collective-permute-start(bf16[192,2048]{1,0:T(8,128)(2,1)S(1)} %constant_dynamic-update-slice_fusion.5), channel_id=1, source_target_pairs={{0,24},{8,0},{16,8},{24,16},{1,25},{9,1},{17,9},{25,17},{2,26},{10... | collective-permute-start | bytes 2359304 | tf_op jit(solution)/shard_map/down_gather/ppermute | solution.py:24
  58.3 32.7 %all-to-all-start = ((bf16[8,192,256]{2,1,0:T(8,128)(2,1)}), bf16[8,192,256]{2,1,0:T(8,128)(2,1)S(1)}, u32[]{:S(2)}, u32[]{:S(2)}) async-start(bf16[8,192,256]{2,1,0:T(8,128)(2,1)} %down_sum_x.1), calls=%async_computation | async-start | bytes 1572864 | tf_op jit(solution)/shard_map/down_z/all_to_all | solution.py:244
  69.1 13.2 %collective-permute-start.13 = (bf16[192,1024]{1,0:T(8,128)(2,1)S(1)}, bf16[192,1024]{1,0:T(8,128)(2,1)S(1)}, u32[]{:S(2)}, u32[]{:S(2)}) collective-permute-start(bf16[192,1024]{1,0:T(8,128)(2,1)S(1)} %slice.24), channel_id=1, source_target_pairs={{0,8},{8,16},{16,24},{24,0},{1,9},{9,17},{17,25},{25,1},{2,10},{10... | collective-permute-start | bytes 1179656 | tf_op jit(solution)/shard_map/down_gather/ppermute | solution.py:24
  70.3 12.1 %collective-permute-start.14 = (bf16[192,1024]{1,0:T(8,128)(2,1)S(1)}, bf16[192,1024]{1,0:T(8,128)(2,1)S(1)}, u32[]{:S(2)}, u32[]{:S(2)}) collective-permute-start(bf16[192,1024]{1,0:T(8,128)(2,1)S(1)} %slice.25), channel_id=1, source_target_pairs={{0,24},{8,0},{16,8},{24,16},{1,25},{9,1},{17,9},{25,17},{2,26},{10... | collective-permute-start | bytes 1179656 | tf_op jit(solution)/shard_map/down_gather/ppermute | solution.py:24
  82.4 1.7 copy-start.1
  91.0 7.0 %copy-start.4 = (bf16[8,192,256]{2,1,0:T(8,128)(2,1)}, bf16[8,192,256]{2,1,0:T(8,128)(2,1)S(1)}, u32[]{:S(2)}) copy-start(bf16[8,192,256]{2,1,0:T(8,128)(2,1)S(1)} %all-to-all-done.parts) | copy-start | bytes 2359300
  91.0 17.3 %all-to-all-start.1 = ((bf16[32,48,128]{2,1,0:T(8,128)(2,1)}), bf16[32,48,128]{2,1,0:T(8,128)(2,1)S(1)}, u32[]{:S(2)}, u32[]{:S(2)}) async-start(bf16[32,48,128]{2,1,0:T(8,128)(2,1)} %up_terms.1), calls=%async_computation.1 | async-start | bytes 786432 | tf_op jit(solution)/shard_map/up_tensor/all_to_all | solution.py:267
  108.3 0.7 copy-start.5
  134.4 0.9 copy-start.2
  137.9 29.8 %all-to-all-start.2 = ((bf16[32,96,128]{2,1,0:T(8,128)(2,1)}), bf16[32,96,128]{2,1,0:T(8,128)(2,1)S(1)}, u32[]{:S(2)}, u32[]{:S(2)}) async-start(bf16[32,96,128]{2,1,0:T(8,128)(2,1)} %get-tuple-element.25), calls=%async_computation.2 | async-start | bytes 1572864 | tf_op jit(solution)/shard_map/up_spread/all_to_all | solution.py:289
  167.6 2.4 %copy-start.3 = (bf16[32,96,128]{2,1,0:T(8,128)(2,1)}, bf16[32,96,128]{2,1,0:T(8,128)(2,1)S(1)}, u32[]{:S(2)}) copy-start(bf16[32,96,128]{2,1,0:T(8,128)(2,1)S(1)} %all-to-all-done.2.mine) | copy-start | bytes 2359300
  167.6 2.4 %collective-permute-start.15 = (bf16[32,96,128]{2,1,0:T(8,128)(2,1)S(1)}, bf16[32,96,128]{2,1,0:T(8,128)(2,1)S(1)}, u32[]{:S(2)}, u32[]{:S(2)}) collective-permute-start(bf16[32,96,128]{2,1,0:T(8,128)(2,1)S(1)} %all-to-all-done.2.mine), channel_id=1, source_target_pairs={{0,32},{32,0},{1,33},{33,1},{2,34},{34,2},{3,35},{35,3},{4,36},{36... | collective-permute-start | bytes 2359304 | tf_op jit(solution)/shard_map/up_swap/ppermute | solution.py:306
  170.0 0.9 copy-start.6
Sparse Core Ops, SparseCore 0:
  11.7 144.4 all-gather.2
